TPU v7x, 32 devices: a whole 2x2x4 slice. The times are simulated.
32 devices in a mesh: dp: 4 (over y, core), row: 2 (over x), col: 4 (over z).
Axes of the slice: x: 2, y: 2, z: 4, core: 2. Of those that a mesh axis runs over, the one named last changes fastest.
Arguments:
- gate_pre: bfloat16 [512, 14336], P('dp', 'row'), may hold values from -6 to 6
- up_pre: bfloat16 [512, 14336], P('dp', 'row'), may hold values from -6 to 6
- down_weight: bfloat16 [14336, 4096], P('row', 'col'), may hold values from -0.046875 to 0.046875
- cotangent: bfloat16 [512, 4096], P(('dp', 'row'), 'col'), may hold values from -6 to 6
Outputs:
- mixed: bfloat16 [512, 4096], P(('dp', 'row'), 'col')
- gate_grad: bfloat16 [512, 14336], P(('dp', 'col'), 'row')
- up_grad: bfloat16 [512, 14336], P(('dp', 'col'), 'row')
- weight_grad: float32 [14336, 4096], P(('row', 'dp'), 'col')
All inputs are finite; a program needn't handle non-finite values.
Results may differ from a plain program's by a relative error of at most 0.017.
Values may be sent and summed in bfloat16 or wider, within the bound.
No kernel may reach another device: no remote copies, remote signals or barrier semaphores. Data moves between devices by JAX's collectives and lax.ppermute only.
A program may use at most 128 MiB of HBM per device.

v0:
```python
import jax
import jax.numpy as jnp
from jax import lax
from jax.sharding import PartitionSpec as P


def body(gate_pre, up_pre, down_weight, cotangent):
    gate_float = gate_pre.astype(jnp.float32)
    up_float = up_pre.astype(jnp.float32)
    sigmoid_gate = jax.nn.sigmoid(gate_float)
    activated = gate_float * sigmoid_gate
    hidden = (activated * up_float).astype(jnp.bfloat16)
    tok_count = hidden.shape[0]
    rows_taken = hidden
    mixed = lax.psum_scatter(
        jnp.dot(rows_taken, down_weight, preferred_element_type=jnp.float32),
        "row",
        scatter_dimension=0,
        tiled=True,
    ).astype(jnp.bfloat16)
    cot_full = lax.all_gather(cotangent, "row", axis=0, tiled=True)
    tok_rows = tok_count // lax.axis_size("col")
    rows_taken = cot_full
    hidden_share = lax.psum_scatter(
        lax.dot_general(
            rows_taken, down_weight, (((1,), (1,)), ((), ())), preferred_element_type=jnp.float32
        ).astype(jnp.bfloat16),
        "col",
        scatter_dimension=0,
        tiled=True,
    ).astype(jnp.float32)
    offset = lax.axis_index("col") * tok_rows
    gate_rows = lax.dynamic_slice_in_dim(gate_float, offset, tok_rows, 0)
    up_rows = lax.dynamic_slice_in_dim(up_float, offset, tok_rows, 0)
    sigmoid_rows = lax.dynamic_slice_in_dim(sigmoid_gate, offset, tok_rows, 0)
    activated_rows = lax.dynamic_slice_in_dim(activated, offset, tok_rows, 0)
    gate_grad = (
        hidden_share * up_rows * sigmoid_rows * (1.0 + gate_rows * (1.0 - sigmoid_rows))
    ).astype(jnp.bfloat16)
    up_grad = (hidden_share * activated_rows).astype(jnp.bfloat16)
    replicas = lax.axis_size("dp")
    grad_total = lax.psum_scatter(
        lax.dot_general(
            hidden, cot_full, (((0,), (0,)), ((), ())), preferred_element_type=jnp.float32
        ),
        "dp",
        scatter_dimension=0,
        tiled=True,
    )
    weight_grad = grad_total / jnp.float32(replicas)
    return (mixed, gate_grad, up_grad, weight_grad)


def solution(mesh):
    placed = (P("dp", "row"), P("dp", "row"), P("row", "col"), P(("dp", "row"), "col"))
    return jax.shard_map(
        body,
        mesh=mesh,
        in_specs=placed,
        out_specs=(
            P(("dp", "row"), "col"),
            P(("dp", "col"), "row"),
            P(("dp", "col"), "row"),
            P(("row", "dp"), "col"),
        ),
        check_vma=False,
    )
```

profile of v0, /device:TPU:0, one launch (start us, length us, event | category | flops | bytes accessed | tf_op | source)
XLA Modules:
  0.0 301.0 jit_solution(5609814526549700776)
XLA Ops:
  7.2 0.0 copy-start.2
  7.2 0.0 reduce-scatter.4.cloned.1.call-start
  7.2 9.7 %fusion.5 = f32[128,1024]{1,0:T(8,128)} fusion(bf16[7168,1024]{1,0:T(8,128)(2,1)} %param.6, bf16[128,7168]{1,0:T(8,128)(2,1)} %param.5, bf16[128,7168]{1,0:T(8,128)(2,1)} %param.4), kind=kOutput, calls=%fused_computation.12 | convolution fusion | flops 1886388224 | bytes 18874368 | tf_op jit(solution)/shard_map/dot_general | solution.py:16
  16.9 0.0 reduce-scatter.4.cloned.1.call-update
  16.9 0.0 reduce-scatter.6.cloned.1.call-start
  17.0 0.0 copy-done.2
  17.0 7.1 %all_gather.3 = bf16[128,1024]{1,0:T(8,128)(2,1)S(1)} all-gather(bf16[64,1024]{1,0:T(8,128)(2,1)S(1)} %copy-done.2), channel_id=1, replica_groups=mesh['dp'=4,'row'=2,'col'=4] {'row'}, dimensions={0}, use_global_device_ids=true | all-gather | bytes 393216 | tf_op jit(solution)/shard_map/all_gather | solution.py:21
  24.1 0.0 copy-start
  24.1 11.6 %convolution_convert_fusion = bf16[128,7168]{1,0:T(8,128)(2,1)} fusion(bf16[128,1024]{1,0:T(8,128)(2,1)S(1)} %all_gather.3, bf16[7168,1024]{1,0:T(8,128)(2,1)} %param.6), kind=kOutput, calls=%fused_computation | convolution fusion | flops 1879965696 | bytes 16777216 | tf_op jit(solution)/shard_map/dot_general | solution.py:25
  35.7 0.0 reduce-scatter.6.cloned.1.call-update
  35.7 0.0 reduce-scatter.8.cloned.1.call-start
  35.8 0.0 copy-done
  35.8 13.6 %fusion.4 = f32[7168,1024]{1,0:T(8,128)} fusion(bf16[128,1024]{1,0:T(8,128)(2,1)S(1)} %all_gather.3, bf16[128,7168]{1,0:T(8,128)(2,1)} %param.5, bf16[128,7168]{1,0:T(8,128)(2,1)S(1)} %copy-done), kind=kOutput, calls=%fused_computation.11 | convolution fusion | flops 1886388224 | bytes 33292288 | tf_op jit(solution)/shard_map/dot_general | solution.py:43
  49.3 0.0 reduce-scatter.8.cloned.1.call-update
  49.4 0.0 copy-start.1
  49.4 2.2 convert_element_type.24
  51.6 0.0 copy-done.1
  51.6 2.3 convert_element_type.25
  53.9 4.2 %convert_multiply_fusion = (f32[128,7168]{1,0:T(8,128)}, f32[128,7168]{1,0:T(8,128)}) fusion(bf16[128,7168]{1,0:T(8,128)(2,1)S(1)} %copy-done), kind=kLoop, calls=%fused_computation.4 | loop fusion | flops 4587520 | bytes 9175040 | tf_op jit(solution)/shard_map/mul | solution.py:11
  58.1 0.0 reduce-scatter.4.cloned.1.call-done
  58.1 1.6 convert_element_type.27
  59.7 17.1 %reduce-scatter.6.cloned.1.call-done = bf16[32,7168]{1,0:T(8,128)(2,1)} async-done(((bf16[128,7168]{1,0:T(8,128)(2,1)}), bf16[32,7168]{1,0:T(8,128)(2,1)}) %reduce-scatter.6.cloned.1.call-update) | async-done | bytes 458768 | tf_op jit(solution)/shard_map/reduce_scatter | solution.py:24
  76.8 3.3 %fusion.3 = (bf16[32,7168]{1,0:T(8,128)(2,1)}, bf16[32,7168]{1,0:T(8,128)(2,1)}) fusion(bf16[32,7168]{1,0:T(8,128)(2,1)} %reduce-scatter.6.cloned.1.call-done, f32[128,7168]{1,0:T(8,128)} %get-tuple-element.4, s32[]{:T(128)S(6)} %select_n.2, f32[128,7168]{1,0:T(8,128)} %convert_element_type.24, f32[128,7168]{1,0:T(8,128)} %get-tuple-element.5, ...), kind=kLoop, calls=%fused_computation.10 | loop fusion | flops 2293760 | bytes 5046276 | tf_op jit(solution)/shard_map/convert_element_type | solution.py:40
  80.2 206.5 %reduce-scatter.8.cloned.1.call-done = f32[1792,1024]{1,0:T(8,128)} async-done(((f32[7168,1024]{1,0:T(8,128)}), f32[1792,1024]{1,0:T(8,128)}) %reduce-scatter.8.cloned.1.call-update) | async-done | bytes 7340048 | tf_op jit(solution)/shard_map/reduce_scatter | solution.py:42
  286.7 7.8 %broadcast_multiply_fusion = f32[1792,1024]{1,0:T(8,128)} fusion(f32[1792,1024]{1,0:T(8,128)} %reduce-scatter.8.cloned.1.call-done), kind=kLoop, calls=%fused_computation.1 | loop fusion | flops 1835008 | bytes 14680064 | tf_op jit(solution)/shard_map/div | solution.py:50
Async XLA Ops:
  7.2 9.8 %copy-start.2 = (bf16[64,1024]{1,0:T(8,128)(2,1)S(1)}, bf16[64,1024]{1,0:T(8,128)(2,1)}, u32[]{:S(2)}) copy-start(bf16[64,1024]{1,0:T(8,128)(2,1)} %param.7) | copy-start | bytes 393220
  7.2 50.9 %reduce-scatter.4.cloned.1.call-start = ((), (), s32[]{:S(2)}) async-start(), calls=%async_computation.3 | async-start | bytes 786432 | tf_op jit(solution)/shard_map/reduce_scatter | solution.py:15
  16.9 59.9 %reduce-scatter.6.cloned.1.call-start = ((), (), s32[]{:S(2)}) async-start(), calls=%async_computation.4 | async-start | bytes 2293760 | tf_op jit(solution)/shard_map/reduce_scatter | solution.py:24
  24.1 11.7 %copy-start = (bf16[128,7168]{1,0:T(8,128)(2,1)S(1)}, bf16[128,7168]{1,0:T(8,128)(2,1)}, u32[]{:S(2)}) copy-start(bf16[128,7168]{1,0:T(8,128)(2,1)} %param.4) | copy-start | bytes 5505028
  35.7 251.0 %reduce-scatter.8.cloned.1.call-start = ((), (), s32[]{:S(2)}) async-start(), calls=%async_computation.5 | async-start | bytes 36700160 | tf_op jit(solution)/shard_map/reduce_scatter | solution.py:42
  49.4 2.2 copy-start.1
Sparse Core Ops, SparseCore 0:
  17.0 17.2 reduce-scatter.3
  36.7 40.0 reduce-scatter.5
  79.6 207.0 reduce-scatter.7
where the time goes:
time: 301 us
  waiting for transfers between devices  224 us (74%)
  matrix products  34.9 us (12%)
  other arithmetic  21.4 us (7%)
  between operations  13.8 us (5%)
  blocking collectives  7.09 us (2%)
    reduce_scatter x1, waiting for transfers between devices, body(): lax.psum_scatter(lax.dot_general(hidden, cot_full, (((0,), (0,)), ((), ()...  207 us
    reduce_scatter x1, waiting for transfers between devices, body(): lax.psum_scatter(lax.dot_general(rows_taken, down_weight, (((1,), (1,)),...  17.1 us
    dot_general x1, matrix products, body(): lax.dot_general(hidden, cot_full, (((0,), (0,)), ((), ())), preferred_ele...  13.6 us
    dot_general x1, matrix products, body(): lax.dot_general(rows_taken, down_weight, (((1,), (1,)), ((), ())), prefer...  11.6 us
    dot_general x1, matrix products, body(): jnp.dot(rows_taken, down_weight, preferred_element_type=jnp.float32)  9.66 us
    div x1, other arithmetic, body(): weight_grad = grad_total / jnp.float32(replicas)  7.78 us
    all_gather x1, blocking collectives, body(): cot_full = lax.all_gather(cotangent, 'row', axis=0, tiled=True)  7.09 us
  transfers between devices with their start and end apart: 3, of which 2 were waited for; matrix products, arithmetic and copies ran while one was open for 13% of the time, Pallas kernels for 0%

commit v1 on v0

v1 whole, which is shorter than its diff:
```python
import jax
import jax.numpy as jnp
from jax import lax
from jax.sharding import PartitionSpec as P

SEND_ORDER = ((3, 2, 1, 0), (2, 0, 3, 1), (1, 3, 0, 2), (0, 1, 2, 3))
FAR_ENDS = ((0, 1), (3, 2))
MIDDLE = ((1, 2), (2, 1))
ROUND_TWO = ((0, 2), (2, 3), (3, 1), (1, 0))
ROUND_THREE = ((0, 1), (1, 3), (3, 2), (2, 0))


def gather_rows(cotangent):
    if lax.axis_size("row") != 2:
        return lax.all_gather(cotangent, "row", axis=0, tiled=True)
    other = lax.ppermute(cotangent, "row", [(0, 1), (1, 0)])
    first = lax.axis_index("row") == 0
    return jnp.concatenate(
        [jnp.where(first, cotangent, other), jnp.where(first, other, cotangent)], axis=0
    )


def scatter_rows(partial):
    if lax.axis_size("row") != 2:
        return lax.psum_scatter(partial, "row", scatter_dimension=0, tiled=True)
    half = partial.shape[0] // 2
    me = lax.axis_index("row")
    mine = lax.dynamic_slice_in_dim(partial, me * half, half, 0)
    theirs = lax.dynamic_slice_in_dim(partial, (1 - me) * half, half, 0)
    return mine + lax.ppermute(theirs, "row", [(0, 1), (1, 0)])


def hidden_gradient(cot_full, down_weight):
    def product(rows):
        return lax.dot_general(
            rows, down_weight, (((1,), (1,)), ((), ())), preferred_element_type=jnp.float32
        ).astype(jnp.bfloat16)

    if lax.axis_size("col") != 4:
        return lax.psum_scatter(
            product(cot_full), "col", scatter_dimension=0, tiled=True
        ).astype(jnp.float32)
    tokens = cot_full.shape[0] // 4
    order = jnp.asarray(SEND_ORDER, jnp.int32)[lax.axis_index("col")]
    blocks = [
        lax.dynamic_slice_in_dim(cot_full, order[i] * tokens, tokens, 0) for i in range(4)
    ]
    partial = product(jnp.concatenate(blocks, axis=0)).reshape(4, tokens, -1)
    transit = lax.ppermute(partial[0], "col", FAR_ENDS)
    middle = lax.ppermute(partial[0], "col", MIDDLE)
    second = lax.ppermute(partial[1], "col", ROUND_TWO)
    forward = (partial[2].astype(jnp.float32) + transit.astype(jnp.float32)).astype(jnp.bfloat16)
    third = lax.ppermute(forward, "col", ROUND_THREE)
    return (
        partial[3].astype(jnp.float32)
        + middle.astype(jnp.float32)
        + second.astype(jnp.float32)
        + third.astype(jnp.float32)
    )


def exchange_replicas(hidden, cot_full):
    if lax.axis_size("dp") != 4:
        return (
            lax.all_to_all(hidden, "dp", split_axis=1, concat_axis=0, tiled=True),
            lax.all_gather(cot_full, "dp", axis=0, tiled=True),
        )
    shard = hidden.shape[1] // 4
    me = lax.axis_index("dp")
    chip, core = me // 2, me % 2
    far = [(i, i ^ 2) for i in range(4)]
    near = [(i, i ^ 1) for i in range(4)]

    def part(index):
        return lax.dynamic_slice_in_dim(hidden, index * shard, shard, 1)

    from_far = lax.ppermute(
        lax.dynamic_slice_in_dim(hidden, (1 - chip) * 2 * shard, 2 * shard, 1), "dp", far
    )
    cot_far = lax.ppermute(cot_full, "dp", far)
    pair = jnp.concatenate([part(me), lax.dynamic_slice_in_dim(from_far, core * shard, shard, 1)], axis=0)
    to_near = jnp.concatenate(
        [part(me ^ 1), lax.dynamic_slice_in_dim(from_far, (1 - core) * shard, shard, 1)], axis=0
    )
    from_near = lax.ppermute(to_near, "dp", near)
    cot_pair = jnp.concatenate([cot_full, cot_far], axis=0)
    cot_near = lax.ppermute(cot_pair, "dp", near)
    return (
        jnp.concatenate([pair, from_near], axis=0),
        jnp.concatenate([cot_pair, cot_near], axis=0),
    )


def body(gate_pre, up_pre, down_weight, cotangent):
    gate_float = gate_pre.astype(jnp.float32)
    hidden = (gate_float * jax.nn.sigmoid(gate_float) * up_pre.astype(jnp.float32)).astype(
        jnp.bfloat16
    )
    cot_full = gather_rows(cotangent)
    hidden_share = hidden_gradient(cot_full, down_weight)
    mixed = scatter_rows(
        jnp.dot(hidden, down_weight, preferred_element_type=jnp.float32)
    ).astype(jnp.bfloat16)

    hidden_all, cot_all = exchange_replicas(hidden, cot_full)
    replicas = lax.axis_size("dp")
    weight_grad = lax.dot_general(
        hidden_all, cot_all, (((0,), (0,)), ((), ())), preferred_element_type=jnp.float32
    ) / jnp.float32(replicas)

    tok_rows = gate_pre.shape[0] // lax.axis_size("col")
    offset = lax.axis_index("col") * tok_rows
    gate_rows = lax.dynamic_slice_in_dim(gate_pre, offset, tok_rows, 0).astype(jnp.float32)
    up_rows = lax.dynamic_slice_in_dim(up_pre, offset, tok_rows, 0).astype(jnp.float32)
    sigmoid_rows = jax.nn.sigmoid(gate_rows)
    gate_grad = (
        hidden_share * up_rows * sigmoid_rows * (1.0 + gate_rows * (1.0 - sigmoid_rows))
    ).astype(jnp.bfloat16)
    up_grad = (hidden_share * gate_rows * sigmoid_rows).astype(jnp.bfloat16)
    return (mixed, gate_grad, up_grad, weight_grad)


def solution(mesh):
    placed = (P("dp", "row"), P("dp", "row"), P("row", "col"), P(("dp", "row"), "col"))
    return jax.shard_map(
        body,
        mesh=mesh,
        in_specs=placed,
        out_specs=(
            P(("dp", "row"), "col"),
            P(("dp", "col"), "row"),
            P(("dp", "col"), "row"),
            P(("row", "dp"), "col"),
        ),
        check_vma=False,
    )
```

time: 301 us -> 80.6 us (0.27)
  waiting for transfers between devices: 224 us -> 20.7 us
  starting transfers between devices: 0.12 us -> 14.6 us
  matrix products: 34.9 us -> 23.4 us
  other arithmetic: 21.4 us -> 10.9 us
  between operations: 13.8 us -> 3.36 us
  local copies, waits for them, and re-layouts: 0.01 us -> 7.15 us
  blocking collectives: 7.09 us -> 0 us
    reduce_scatter x3 -> x0, waiting for transfers between devices: 224 us -> none  [the longest x1 207 us: body(): lax.psum_scatter(lax.dot_general(hidden, cot_full, (((0,), (0,)), ((), ()...]
    ppermute x0 -> x10, waiting for transfers between devices: none -> 20.7 us  [the longest x1 11.4 us: hidden_gradient(): third = lax.ppermute(forward, 'col', ROUND_THREE)]
    ppermute x0 -> x10, starting transfers between devices: none -> 14.6 us  [the longest x1 4.76 us: hidden_gradient(): transit = lax.ppermute(partial[0], 'col', FAR_ENDS)]
    dot_general x3, matrix products: 34.9 us -> 23.4 us  [the longest x1 10 us: product(): lax.dot_general(rows, down_weight, (((1,), (1,)), ((), ())), preferred_el...]
    div x1 -> x0, other arithmetic: 7.78 us -> none  [body(): weight_grad = grad_total / jnp.float32(replicas)]
    all_gather x1 -> x0, blocking collectives: 7.09 us -> none  [body(): cot_full = lax.all_gather(cotangent, 'row', axis=0, tiled=True)]
    dynamic_slice x0 -> x5, local copies, waits for them, and re-layouts: none -> 4.45 us  [the longest x1 1.22 us: exchange_replicas(): lax.dynamic_slice_in_dim(from_far, core * shard, shard, 1)]
    mul x1 -> x0, other arithmetic: 4.24 us -> none  [body(): activated = gate_float * sigmoid_gate]
  transfers between devices with their start and end apart: 3 -> 10, of which waited for: 2 -> 3; matrix products, arithmetic and copies ran while one was open for 13% -> 43% of each run, Pallas kernels for 0% -> 0%
where the time goes in v1:
time: 80.6 us; the launch traced here: 80.1 us
  matrix products  23.4 us (29%)
  waiting for transfers between devices  20.7 us (26%)
  starting transfers between devices  14.6 us (18%)
  other arithmetic  10.9 us (14%)
  local copies, waits for them, and re-layouts  7.15 us (9%)
  between operations  3.36 us (4%)
    ppermute x1, waiting for transfers between devices, hidden_gradient(): third = lax.ppermute(forward, 'col', ROUND_THREE)  11.4 us
    dot_general x1, matrix products, product(): lax.dot_general(rows, down_weight, (((1,), (1,)), ((), ())), preferred_el...  10 us
    dot_general x1, matrix products, body(): jnp.dot(hidden, down_weight, preferred_element_type=jnp.float32)  7.23 us
    dot_general x1, matrix products, body(): lax.dot_general(hidden_all, cot_all, (((0,), (0,)), ((), ())), preferred_...  6.11 us
    ppermute x1, starting transfers between devices, hidden_gradient(): transit = lax.ppermute(partial[0], 'col', FAR_ENDS)  4.76 us
    ppermute x1, waiting for transfers between devices, hidden_gradient(): second = lax.ppermute(partial[1], 'col', ROUND_TWO)  4.69 us
    ppermute x1, waiting for transfers between devices, hidden_gradient(): transit = lax.ppermute(partial[0], 'col', FAR_ENDS)  4.59 us
    convert_element_type x1, other arithmetic, body(): (gate_float * jax.nn.sigmoid(gate_float) * up_pre.astype(jnp.float32)).as...  3.13 us
  transfers between devices with their start and end apart: 10, of which 3 were waited for; matrix products, arithmetic and copies ran while one was open for 43% of the time, Pallas kernels for 0%

profile of v1, /device:TPU:0, one launch (start us, length us, event | category | flops | bytes accessed | tf_op | source)
XLA Modules:
  0.0 80.1 jit_solution(4028724683611380301)
XLA Ops:
  0.6 3.0 %collective-permute-start.1 = (bf16[64,1024]{1,0:T(8,128)(2,1)}, bf16[64,1024]{1,0:T(8,128)(2,1)S(1)}, u32[]{:S(2)}, u32[]{:S(2)}) collective-permute-start(bf16[64,1024]{1,0:T(8,128)(2,1)} %param.8), channel_id=1, source_target_pairs={{0,4},{4,0},{1,5},{5,1},{2,6},{6,2},{3,7},{7,3},{8,12},{12,8},{9,1... | collective-permute-start | bytes 393224 | tf_op jit(solution)/shard_map/ppermute | solution.py:16
  3.6 3.1 %fusion.4 = bf16[128,7168]{1,0:T(8,128)(2,1)S(1)} fusion(bf16[128,7168]{1,0:T(8,128)(2,1)} %param.6, bf16[128,7168]{1,0:T(8,128)(2,1)} %param.5), kind=kLoop, calls=%fused_computation.8 | loop fusion | flops 7340032 | bytes 5505024 | tf_op jit(solution)/shard_map/convert_element_type | solution.py:96
  6.8 7.2 %fusion.40 = f32[128,1024]{1,0:T(8,128)S(1)} fusion(bf16[128,7168]{1,0:T(8,128)(2,1)S(1)} %fusion.4, bf16[7168,1024]{1,0:T(8,128)(2,1)} %param.7), kind=kOutput, calls=%fused_computation.70 | convolution fusion | flops 1879048192 | bytes 17039360 | tf_op jit(solution)/shard_map/dot_general | solution.py:102
  14.0 0.0 copy-start.2
  14.0 0.7 constant_dynamic-slice_fusion.6
  14.8 0.0 collective-permute-start
  14.8 1.0 %constant_dynamic-slice_fusion.3 = bf16[128,3584]{1,0:T(8,128)(2,1)} fusion(bf16[128,7168]{1,0:T(8,128)(2,1)S(1)} %fusion.4, s32[]{:T(128)S(6)} %select_n.76), kind=kLoop, calls=%fused_computation.62 | loop fusion | bytes 1835012 | tf_op jit(solution)/shard_map/dynamic_slice | solution.py:78
  15.8 2.0 %collective-permute-start.6 = (bf16[128,3584]{1,0:T(8,128)(2,1)}, bf16[128,3584]{1,0:T(8,128)(2,1)}, u32[]{:S(2)}, u32[]{:S(2)}) collective-permute-start(bf16[128,3584]{1,0:T(8,128)(2,1)} %constant_dynamic-slice_fusion.3), channel_id=1, source_target_pairs={{0,16},{8,24},{16,0},{24,8},{1,17},{9,25},{17,1},{25,9},{2,18},{10... | collective-permute-start | bytes 2752520 | tf_op jit(solution)/shard_map/ppermute | solution.py:77
  17.8 0.7 constant_dynamic-slice_fusion.5
  18.5 0.6 fusion.39
  21.7 0.0 collective-permute-done.1
  21.7 0.0 copy-done.2
  21.8 0.7 pad_maximum_fusion.2
  22.5 0.0 collective-permute-start.8
  22.5 0.2 fusion.32
  22.7 10.0 %convolution_convert_fusion = bf16[128,7168]{1,0:T(8,128)(2,1)S(1)} fusion(bf16[7168,1024]{1,0:T(8,128)(2,1)} %param.7, bf16[32,1024]{1,0:T(8,128)(2,1)S(1)} %get-tuple-element.15, bf16[32,1024]{1,0:T(8,128)(2,1)S(1)} %get-tuple-element.14, bf16[32,1024]{1,0:T(8,128)(2,1)S(1)} %get-tuple-element.13, bf16[32,1024]{1,0:T(8,128)(2,1)S(1)} %get-tuple-element.12), kind=kOutput, calls=%fused_computation | convolution fusion | flops 1881014272 | bytes 16777216 | tf_op jit(solution)/shard_map/dot_general | solution.py:35
  32.8 0.0 copy-start
  32.8 1.2 %copy-done = bf16[128,7168]{1,0:T(8,128)(2,1)} copy-done((bf16[128,7168]{1,0:T(8,128)(2,1)}, bf16[128,7168]{1,0:T(8,128)(2,1)S(1)}, u32[]{:S(2)}) %copy-start) | copy-done | bytes 1835032
  34.0 0.8 %fusion.38 = (bf16[32,7168]{1,0:T(8,128)(2,1)}, bf16[32,7168]{1,0:T(8,128)(2,1)S(1)}) fusion(bf16[128,7168]{1,0:T(8,128)(2,1)S(1)} %convolution_convert_fusion), kind=kLoop, calls=%fused_computation.68 | loop fusion | bytes 1835008 | tf_op jit(solution)/shard_map/slice | solution.py:51
  34.8 4.8 %collective-permute-start.4 = (bf16[32,7168]{1,0:T(8,128)(2,1)S(1)}, bf16[32,7168]{1,0:T(8,128)(2,1)}, u32[]{:S(2)}, u32[]{:S(2)}) collective-permute-start(bf16[32,7168]{1,0:T(8,128)(2,1)S(1)} %get-tuple-element.9), channel_id=1, source_target_pairs={{0,1},{3,2},{4,5},{7,6},{8,9},{11,10},{12,13},{15,14},{16,17},{19,... | collective-permute-start | bytes 1376264 | tf_op jit(solution)/shard_map/ppermute | solution.py:49
  39.6 0.8 %constant_dynamic-slice_fusion.4 = (bf16[128,1792]{1,0:T(8,128)(2,1)}, bf16[128,1792]{1,0:T(8,128)(2,1)S(1)}) fusion(bf16[128,7168]{1,0:T(8,128)(2,1)S(1)} %fusion.4, s32[]{:T(128)S(6)} %select_n.74, s32[]{:T(128)S(6)} %select_n.79), kind=kLoop, calls=%fused_computation.63 | loop fusion | bytes 1835016 | tf_op jit(solution)/shard_map/dynamic_slice | solution.py:75
  40.4 0.7 collective-permute-start.2
  41.1 0.0 collective-permute-done
  41.1 1.4 %collective-permute-start.3 = (bf16[32,7168]{1,0:T(8,128)(2,1)}, bf16[32,7168]{1,0:T(8,128)(2,1)S(1)}, u32[]{:S(2)}, u32[]{:S(2)}) collective-permute-start(bf16[32,7168]{1,0:T(8,128)(2,1)} %get-tuple-element.8), channel_id=1, source_target_pairs={{0,2},{2,3},{3,1},{1,0},{4,6},{6,7},{7,5},{5,4},{8,10},{10,11},{11... | collective-permute-start | bytes 1376264 | tf_op jit(solution)/shard_map/ppermute | solution.py:51
  42.4 1.6 %add_convert_fusion.1 = bf16[64,1024]{1,0:T(8,128)(2,1)} fusion(f32[64,1024]{1,0:T(8,128)} %collective-permute-done, f32[128,1024]{1,0:T(8,128)S(1)} %fusion.40, s32[]{:T(128)S(6)} %select_n.63), kind=kLoop, calls=%fused_computation.52 | loop fusion | flops 131072 | bytes 655364 | tf_op jit(solution)/shard_map/convert_element_type | solution.py:103
  44.1 0.0 collective-permute-done.8
  44.1 1.0 %pad_maximum_fusion.1 = bf16[256,1024]{1,0:T(8,128)(2,1)S(1)} fusion(bf16[128,1024]{1,0:T(8,128)(2,1)} %collective-permute-done.8, bf16[64,1024]{1,0:T(8,128)(2,1)S(1)} %get-tuple-element.16, bf16[64,1024]{1,0:T(8,128)(2,1)S(1)} %get-tuple-element.17), kind=kLoop, calls=%fused_computation.35 | loop fusion | flops 1572864 | bytes 1048576 | tf_op jit(solution)/shard_map/concatenate | solution.py:86
  45.1 0.1 collective-permute-start.9
  45.1 4.6 %collective-permute-done.4 = bf16[32,7168]{1,0:T(8,128)(2,1)} collective-permute-done((bf16[32,7168]{1,0:T(8,128)(2,1)S(1)}, bf16[32,7168]{1,0:T(8,128)(2,1)}, u32[]{:S(2)}, u32[]{:S(2)}) %collective-permute-start.4) | collective-permute-done | bytes 458784 | tf_op jit(solution)/shard_map/ppermute | solution.py:49
  49.7 1.3 %add_convert_fusion = bf16[32,7168]{1,0:T(8,128)(2,1)S(1)} fusion(bf16[32,7168]{1,0:T(8,128)(2,1)} %collective-permute-done.4, bf16[128,7168]{1,0:T(8,128)(2,1)} %copy-done), kind=kLoop, calls=%fused_computation.34 | loop fusion | flops 917504 | bytes 1376256 | tf_op jit(solution)/shard_map/convert_element_type | solution.py:52
  51.0 2.6 %collective-permute-start.5 = (bf16[32,7168]{1,0:T(8,128)(2,1)S(1)}, bf16[32,7168]{1,0:T(8,128)(2,1)S(1)}, u32[]{:S(2)}, u32[]{:S(2)}) collective-permute-start(bf16[32,7168]{1,0:T(8,128)(2,1)S(1)} %add_convert_fusion), channel_id=1, source_target_pairs={{0,1},{1,3},{3,2},{2,0},{4,5},{5,7},{7,6},{6,4},{8,9},{9,11},{11,1... | collective-permute-start | bytes 1376264 | tf_op jit(solution)/shard_map/ppermute | solution.py:53
  53.6 0.0 collective-permute-done.6
  53.7 1.2 %constant_dynamic-slice_fusion.2 = (bf16[128,1792]{1,0:T(8,128)(2,1)S(1)}, bf16[128,1792]{1,0:T(8,128)(2,1)S(1)}) fusion(bf16[128,3584]{1,0:T(8,128)(2,1)} %collective-permute-done.6, s32[]{:T(128)S(6)} %select_n.78, s32[]{:T(128)S(6)} %select_n.80), kind=kLoop, calls=%fused_computation.61 | loop fusion | bytes 1835016 | tf_op jit(solution)/shard_map/dynamic_slice | solution.py:81
  54.9 0.1 pad_maximum_fusion
  54.9 0.0 copy-start.1
  55.0 0.1 collective-permute-start.7
  55.0 4.7 %collective-permute-done.3 = bf16[32,7168]{1,0:T(8,128)(2,1)S(1)} collective-permute-done((bf16[32,7168]{1,0:T(8,128)(2,1)}, bf16[32,7168]{1,0:T(8,128)(2,1)S(1)}, u32[]{:S(2)}, u32[]{:S(2)}) %collective-permute-start.3) | collective-permute-done | bytes 458784 | tf_op jit(solution)/shard_map/ppermute | solution.py:51
  59.7 0.0 collective-permute-done.2
  59.7 11.4 %collective-permute-done.5 = bf16[32,7168]{1,0:T(8,128)(2,1)S(1)} collective-permute-done((bf16[32,7168]{1,0:T(8,128)(2,1)S(1)}, bf16[32,7168]{1,0:T(8,128)(2,1)S(1)}, u32[]{:S(2)}, u32[]{:S(2)}) %collective-permute-start.5) | collective-permute-done | bytes 458784 | tf_op jit(solution)/shard_map/ppermute | solution.py:53
  71.1 2.9 %fusion.24 = (bf16[32,7168]{1,0:T(8,128)(2,1)}, bf16[32,7168]{1,0:T(8,128)(2,1)}) fusion(bf16[128,7168]{1,0:T(8,128)(2,1)} %param.5, s32[]{:T(128)S(6)} %select_n.73, bf16[32,7168]{1,0:T(8,128)(2,1)S(1)} %collective-permute-done.5, bf16[32,7168]{1,0:T(8,128)(2,1)S(1)} %collective-permute-done.3, bf16[32,7168]{1,0:T(8,128)(2,1)S(1)} %collective-permute-done.2, ...), kind=kLoop, calls=%fused_computation.31 | loop fusion | flops 5046272 | bytes 3670020 | tf_op jit(solution)/shard_map/convert_element_type | solution.py:119
  74.0 0.0 collective-permute-done.9
  74.0 0.0 collective-permute-done.7
  74.0 0.0 copy-done.1
  74.0 6.1 %convolution_multiply_fusion = f32[1792,1024]{1,0:T(8,128)} fusion(bf16[256,1792]{1,0:T(8,128)(2,1)S(1)} %collective-permute-done.7, bf16[128,1792]{1,0:T(8,128)(2,1)S(1)} %get-tuple-element.10, bf16[128,1792]{1,0:T(8,128)(2,1)S(1)} %copy-done.1, bf16[256,1024]{1,0:T(8,128)(2,1)S(1)} %collective-permute-done.9, ...), kind=kOutput, calls=%fused_computation.3 | convolution fusion | flops 1890582528 | bytes 10223616 | tf_op jit(solution)/shard_map/dot_general | solution.py:107
  (1 shorter events, 0.0 us)
Async XLA Ops:
  0.6 21.1 %collective-permute-start.1 = (bf16[64,1024]{1,0:T(8,128)(2,1)}, bf16[64,1024]{1,0:T(8,128)(2,1)S(1)}, u32[]{:S(2)}, u32[]{:S(2)}) collective-permute-start(bf16[64,1024]{1,0:T(8,128)(2,1)} %param.8), channel_id=1, source_target_pairs={{0,4},{4,0},{1,5},{5,1},{2,6},{6,2},{3,7},{7,3},{8,12},{12,8},{9,1... | collective-permute-start | bytes 393224 | tf_op jit(solution)/shard_map/ppermute | solution.py:16
  14.0 7.7 %copy-start.2 = (bf16[64,1024]{1,0:T(8,128)(2,1)S(1)}, bf16[64,1024]{1,0:T(8,128)(2,1)}, u32[]{:S(2)}) copy-start(bf16[64,1024]{1,0:T(8,128)(2,1)} %param.8) | copy-start | bytes 393220
  14.8 26.3 %collective-permute-start = (f32[64,1024]{1,0:T(8,128)}, f32[64,1024]{1,0:T(8,128)}, u32[]{:S(2)}, u32[]{:S(2)}) collective-permute-start(f32[64,1024]{1,0:T(8,128)} %constant_dynamic-slice_fusion.6), channel_id=1, source_target_pairs={{0,4},{4,0},{1,5},{5,1},{2,6},{6,2},{3,7},{7,3},{8,12},{12,8},{9,1... | collective-permute-start | bytes 786440 | tf_op jit(solution)/shard_map/ppermute | solution.py:30
  15.8 37.9 %collective-permute-start.6 = (bf16[128,3584]{1,0:T(8,128)(2,1)}, bf16[128,3584]{1,0:T(8,128)(2,1)}, u32[]{:S(2)}, u32[]{:S(2)}) collective-permute-start(bf16[128,3584]{1,0:T(8,128)(2,1)} %constant_dynamic-slice_fusion.3), channel_id=1, source_target_pairs={{0,16},{8,24},{16,0},{24,8},{1,17},{9,25},{17,1},{25,9},{2,18},{10... | collective-permute-start | bytes 2752520 | tf_op jit(solution)/shard_map/ppermute | solution.py:77
  22.5 21.6 %collective-permute-start.8 = (bf16[128,1024]{1,0:T(8,128)(2,1)}, bf16[128,1024]{1,0:T(8,128)(2,1)}, u32[]{:S(2)}, u32[]{:S(2)}) collective-permute-start(bf16[128,1024]{1,0:T(8,128)(2,1)} %pad_maximum_fusion.2), channel_id=1, source_target_pairs={{0,16},{8,24},{16,0},{24,8},{1,17},{9,25},{17,1},{25,9},{2,18},{10... | collective-permute-start | bytes 786440 | tf_op jit(solution)/shard_map/ppermute | solution.py:80
  32.8 1.2 %copy-start = (bf16[128,7168]{1,0:T(8,128)(2,1)}, bf16[128,7168]{1,0:T(8,128)(2,1)S(1)}, u32[]{:S(2)}) copy-start(bf16[128,7168]{1,0:T(8,128)(2,1)S(1)} %convolution_convert_fusion) | copy-start | bytes 5505028
  34.8 14.9 %collective-permute-start.4 = (bf16[32,7168]{1,0:T(8,128)(2,1)S(1)}, bf16[32,7168]{1,0:T(8,128)(2,1)}, u32[]{:S(2)}, u32[]{:S(2)}) collective-permute-start(bf16[32,7168]{1,0:T(8,128)(2,1)S(1)} %get-tuple-element.9), channel_id=1, source_target_pairs={{0,1},{3,2},{4,5},{7,6},{8,9},{11,10},{12,13},{15,14},{16,17},{19,... | collective-permute-start | bytes 1376264 | tf_op jit(solution)/shard_map/ppermute | solution.py:49
  40.4 19.3 %collective-permute-start.2 = (bf16[32,7168]{1,0:T(8,128)(2,1)S(1)}, bf16[32,7168]{1,0:T(8,128)(2,1)S(1)}, u32[]{:S(2)}, u32[]{:S(2)}) collective-permute-start(bf16[32,7168]{1,0:T(8,128)(2,1)S(1)} %get-tuple-element.9), channel_id=1, source_target_pairs={{1,2},{2,1},{5,6},{6,5},{9,10},{10,9},{13,14},{14,13},{17,18},{18,... | collective-permute-start | bytes 1376264 | tf_op jit(solution)/shard_map/ppermute | solution.py:50
  41.1 18.6 %collective-permute-start.3 = (bf16[32,7168]{1,0:T(8,128)(2,1)}, bf16[32,7168]{1,0:T(8,128)(2,1)S(1)}, u32[]{:S(2)}, u32[]{:S(2)}) collective-permute-start(bf16[32,7168]{1,0:T(8,128)(2,1)} %get-tuple-element.8), channel_id=1, source_target_pairs={{0,2},{2,3},{3,1},{1,0},{4,6},{6,7},{7,5},{5,4},{8,10},{10,11},{11... | collective-permute-start | bytes 1376264 | tf_op jit(solution)/shard_map/ppermute | solution.py:51
  45.1 28.9 %collective-permute-start.9 = (bf16[256,1024]{1,0:T(8,128)(2,1)S(1)}, bf16[256,1024]{1,0:T(8,128)(2,1)S(1)}, u32[]{:S(2)}, u32[]{:S(2)}) collective-permute-start(bf16[256,1024]{1,0:T(8,128)(2,1)S(1)} %pad_maximum_fusion.1), channel_id=1, source_target_pairs={{0,8},{8,0},{16,24},{24,16},{1,9},{9,1},{17,25},{25,17},{2,10},{10... | collective-permute-start | bytes 1572872 | tf_op jit(solution)/shard_map/ppermute | solution.py:87
  51.0 20.1 %collective-permute-start.5 = (bf16[32,7168]{1,0:T(8,128)(2,1)S(1)}, bf16[32,7168]{1,0:T(8,128)(2,1)S(1)}, u32[]{:S(2)}, u32[]{:S(2)}) collective-permute-start(bf16[32,7168]{1,0:T(8,128)(2,1)S(1)} %add_convert_fusion), channel_id=1, source_target_pairs={{0,1},{1,3},{3,2},{2,0},{4,5},{5,7},{7,6},{6,4},{8,9},{9,11},{11,1... | collective-permute-start | bytes 1376264 | tf_op jit(solution)/shard_map/ppermute | solution.py:53
  54.9 19.1 %copy-start.1 = (bf16[128,1792]{1,0:T(8,128)(2,1)S(1)}, bf16[128,1792]{1,0:T(8,128)(2,1)}, u32[]{:S(2)}) copy-start(bf16[128,1792]{1,0:T(8,128)(2,1)} %get-tuple-element.6) | copy-start | bytes 1376260
  55.0 19.1 %collective-permute-start.7 = (bf16[256,1792]{1,0:T(8,128)(2,1)S(1)}, bf16[256,1792]{1,0:T(8,128)(2,1)S(1)}, u32[]{:S(2)}, u32[]{:S(2)}) collective-permute-start(bf16[256,1792]{1,0:T(8,128)(2,1)S(1)} %pad_maximum_fusion), channel_id=1, source_target_pairs={{0,8},{8,0},{16,24},{24,16},{1,9},{9,1},{17,25},{25,17},{2,10},{10... | collective-permute-start | bytes 2752520 | tf_op jit(solution)/shard_map/ppermute | solution.py:85

commit v2 on v0

v2 whole, which is shorter than its diff:
```python
import functools

import jax
import jax.numpy as jnp
from jax import lax
from jax.experimental import pallas as pl
from jax.experimental.pallas import tpu as pltpu
from jax.sharding import PartitionSpec as P

SEND_ORDER = ((3, 2, 1, 0), (2, 0, 3, 1), (1, 3, 0, 2), (0, 1, 2, 3))
ENDS = ((0, 1), (1, 0), (2, 3), (3, 2))
MIDDLE = ((1, 2), (2, 1))
ROUND_TWO = ((0, 2), (2, 3), (3, 1), (1, 0))
ROUND_THREE = ((0, 1), (1, 3), (3, 2), (2, 0))
SWAP = ((0, 1), (1, 0))
FAR = ((0, 2), (1, 3), (2, 0), (3, 1))
NEAR = ((0, 1), (1, 0), (2, 3), (3, 2))

VMEM = pl.BlockSpec(memory_space=pltpu.VMEM)
HBM = pl.BlockSpec(memory_space=pltpu.HBM)
MIB = 2**20
CHUNK = 896
NO_COST = pl.CostEstimate(flops=0, bytes_accessed=0, transcendentals=0)


def after(value, *earlier):
    return lax.optimization_barrier((value,) + earlier)[0]


def in_hbm(array):
    return pltpu.with_memory_space_constraint(array, pltpu.HBM)


def in_vmem(array):
    return pltpu.with_memory_space_constraint(array, pltpu.VMEM)


def silu_product(gate, up):
    gate = gate.astype(jnp.float32)
    return (gate * jax.nn.sigmoid(gate) * up.astype(jnp.float32)).astype(jnp.bfloat16)


def shard_columns(ref, index, shard):
    return ref.at[:, pl.ds(pl.multiple_of(index * shard, shard), shard)]


def first_kernel(
    gate_hbm, up_hbm, weight_hbm, far_ref, weight_ref, gate_ref, up_ref, weight_sem, gate_sems, up_sems
):
    me = lax.axis_index("dp")
    tokens, shard = gate_ref.shape[1:]
    half = weight_ref.shape[0]

    def gate_copy(i):
        return pltpu.make_async_copy(
            shard_columns(gate_hbm, me ^ (3 - i), shard), gate_ref.at[i], gate_sems.at[i]
        )

    def up_copy(i):
        return pltpu.make_async_copy(
            shard_columns(up_hbm, me ^ (3 - i), shard), up_ref.at[i], up_sems.at[i]
        )

    load = pltpu.make_async_copy(weight_hbm.at[:half], weight_ref, weight_sem.at[0])
    for i in range(2):
        gate_copy(i).start()
        up_copy(i).start()
    load.start()
    for i in range(2):
        gate_copy(i).wait()
        up_copy(i).wait()
        far_ref[i * tokens : (i + 1) * tokens] = silu_product(gate_ref[i], up_ref[i])
    load.wait()


def hidden_far_and_weight(gate_pre, up_pre, down_weight):
    tokens, units = gate_pre.shape
    features = down_weight.shape[1]
    shard = units // 4
    return pl.pallas_call(
        first_kernel,
        in_specs=[HBM] * 3,
        out_specs=[VMEM] * 2,
        out_shape=[jax.ShapeDtypeStruct((2 * tokens, shard), jnp.bfloat16), pltpu.VMEM((units // 2, features), jnp.bfloat16)],
        scratch_shapes=[
            pltpu.VMEM((2, tokens, shard), jnp.bfloat16),
            pltpu.VMEM((2, tokens, shard), jnp.bfloat16),
            pltpu.SemaphoreType.DMA((1,)),
            pltpu.SemaphoreType.DMA((2,)),
            pltpu.SemaphoreType.DMA((2,)),
        ],
        compiler_params=pltpu.CompilerParams(vmem_limit_bytes=24 * MIB),
        cost_estimate=NO_COST,
        name="hidden_far",
    )(in_hbm(gate_pre), in_hbm(up_pre), in_hbm(down_weight))


def hidden_grad_kernel(
    own_ref, other_ref, low_ref, weight_hbm, full_ref, ends, middle, second, third, mine, ordered_ref, high_ref, sem
):
    units = low_ref.shape[0]
    load = pltpu.make_async_copy(weight_hbm.at[units:], high_ref, sem.at[0])
    load.start()
    half = own_ref.shape[0]
    tokens = half // 2
    top = lax.axis_index("row") == 0
    full_ref[:half] = jnp.where(top, own_ref[...], other_ref[...])
    full_ref[half:] = jnp.where(top, other_ref[...], own_ref[...])
    place = lax.axis_index("col")
    for i in range(4):
        block = jnp.int32(SEND_ORDER[0][i])
        for z in range(1, 4):
            block = jnp.where(place == z, jnp.int32(SEND_ORDER[z][i]), block)
        start = pl.multiple_of(block * tokens, tokens)
        ordered_ref[i * tokens : (i + 1) * tokens] = full_ref[pl.ds(start, tokens)]
    size = CHUNK if units % CHUNK == 0 else units
    for base, weight_ref in ((0, low_ref), (units, high_ref)):
        if base:
            load.wait()
        for start in range(0, units, size):
            product = lax.dot_general(
                weight_ref[start : start + size],
                ordered_ref[...],
                (((1,), (1,)), ((), ())),
                preferred_element_type=jnp.float32,
            )
            rounded = product.astype(jnp.bfloat16).T
            columns = slice(base + start, base + start + size)
            ends[:, columns] = rounded[:tokens]
            middle[:, columns] = rounded[:tokens]
            second[:, columns] = rounded[tokens : 2 * tokens]
            third[:, columns] = rounded[2 * tokens : 3 * tokens]
            mine[:, columns] = rounded[3 * tokens :]


def hidden_grad_parts(own, other, low, down_weight):
    half, depth = own.shape
    units = low.shape[0]
    part = jax.ShapeDtypeStruct((half // 2, 2 * units), jnp.bfloat16)
    return pl.pallas_call(
        hidden_grad_kernel,
        in_specs=[VMEM, VMEM, VMEM, HBM],
        out_specs=[VMEM] * 6,
        out_shape=[jax.ShapeDtypeStruct((2 * half, depth), jnp.bfloat16)] + [part] * 5,
        scratch_shapes=[
            pltpu.VMEM((2 * half, depth), jnp.bfloat16),
            pltpu.VMEM((units, depth), jnp.bfloat16),
            pltpu.SemaphoreType.DMA((1,)),
        ],
        compiler_params=pltpu.CompilerParams(vmem_limit_bytes=24 * MIB),
        cost_estimate=NO_COST,
        name="hidden_grad",
    )(own, other, in_vmem(low), in_hbm(down_weight))


def mixed_kernel(
    gate_hbm, up_hbm, weight_hbm, far_ref,
    near_ref, mine_ref, keep_ref, send_ref, gate_factor_ref, up_factor_ref,
    weight_ref, gate_ref, up_ref, gate_rows_ref, up_rows_ref, total_ref,
    weight_sems, gate_sems, up_sems, row_sems,
):
    me = lax.axis_index("dp")
    tokens, shard = mine_ref.shape
    tok_rows = gate_rows_ref.shape[0]
    places = (me ^ 3, me ^ 2, me ^ 1, me)
    refs = (far_ref.at[:tokens], far_ref.at[tokens:], near_ref, mine_ref)

    def gate_copy(i):
        return pltpu.make_async_copy(
            shard_columns(gate_hbm, places[2 + i], shard), gate_ref.at[i], gate_sems.at[i]
        )

    def up_copy(i):
        return pltpu.make_async_copy(
            shard_columns(up_hbm, places[2 + i], shard), up_ref.at[i], up_sems.at[i]
        )

    def weight_copy(i):
        start = pl.multiple_of(places[i] * shard, shard)
        return pltpu.make_async_copy(
            weight_hbm.at[pl.ds(start, shard)], weight_ref.at[i], weight_sems.at[i]
        )

    def row_copy(i):
        start = pl.multiple_of(lax.axis_index("col") * tok_rows, tok_rows)
        source, target = ((gate_hbm, gate_rows_ref), (up_hbm, up_rows_ref))[i]
        return pltpu.make_async_copy(source.at[pl.ds(start, tok_rows)], target, row_sems.at[i])

    for i in range(2):
        gate_copy(i).start()
        up_copy(i).start()
    for i in range(2):
        row_copy(i).start()
    for i in range(4):
        weight_copy(i).start()
    for i in range(2):
        gate_copy(i).wait()
        up_copy(i).wait()
        refs[2 + i][...] = silu_product(gate_ref[i], up_ref[i])
    row_copy(0).wait()
    row_copy(1).wait()
    units = gate_rows_ref.shape[1]
    for start in range(0, units, shard):
        columns = slice(start, start + shard)
        gate = gate_rows_ref[:, columns].astype(jnp.float32)
        sigmoid = jax.nn.sigmoid(gate)
        gate_factor_ref[:, columns] = (
            up_rows_ref[:, columns].astype(jnp.float32) * sigmoid * (1.0 + gate * (1.0 - sigmoid))
        )
        up_factor_ref[:, columns] = gate * sigmoid
    for i in range(4):
        weight_copy(i).wait()
        product = jnp.dot(refs[i][...], weight_ref[i], preferred_element_type=jnp.float32)
        if i == 0:
            total_ref[...] = product
        else:
            total_ref[...] += product
    half = tokens // 2
    row = lax.axis_index("row")
    keep_ref[...] = total_ref[pl.ds(pl.multiple_of(row * half, half), half)]
    send_ref[...] = total_ref[pl.ds(pl.multiple_of((1 - row) * half, half), half)]


def mixed_and_factors(gate_pre, up_pre, down_weight, far):
    tokens, units = gate_pre.shape
    shard = units // 4
    features = down_weight.shape[1]
    tok_rows = tokens // lax.axis_size("col")
    hidden = jax.ShapeDtypeStruct((tokens, shard), jnp.bfloat16)
    partial = jax.ShapeDtypeStruct((tokens // 2, features), jnp.float32)
    factor = jax.ShapeDtypeStruct((tok_rows, units), jnp.float32)
    return pl.pallas_call(
        mixed_kernel,
        in_specs=[HBM] * 3 + [VMEM],
        out_specs=[VMEM] * 6,
        out_shape=[hidden, hidden, partial, partial, factor, factor],
        scratch_shapes=[
            pltpu.VMEM((4, shard, features), jnp.bfloat16),
            pltpu.VMEM((2, tokens, shard), jnp.bfloat16),
            pltpu.VMEM((2, tokens, shard), jnp.bfloat16),
            pltpu.VMEM((tok_rows, units), jnp.bfloat16),
            pltpu.VMEM((tok_rows, units), jnp.bfloat16),
            pltpu.VMEM((tokens, features), jnp.float32),
            pltpu.SemaphoreType.DMA((4,)),
            pltpu.SemaphoreType.DMA((2,)),
            pltpu.SemaphoreType.DMA((2,)),
            pltpu.SemaphoreType.DMA((2,)),
        ],
        compiler_params=pltpu.CompilerParams(vmem_limit_bytes=32 * MIB),
        cost_estimate=NO_COST,
        name="mixed",
    )(in_hbm(gate_pre), in_hbm(up_pre), in_hbm(down_weight), far)


def weight_grad_kernel(scale, mine, far, near, both, cot_own, cot_far, cot_near, out):
    tokens = mine.shape[0]
    hidden = jnp.concatenate([mine[...], far[tokens:], near[...], both[...]], axis=0)
    cotangent = jnp.concatenate([cot_own[...], cot_far[...], cot_near[...]], axis=0)
    out[...] = lax.dot_general(
        hidden, cotangent, (((0,), (0,)), ((), ())), preferred_element_type=jnp.float32
    ) * jnp.float32(scale)


def weight_grad_shard(mine, far, near, both, cot_own, cot_far, cot_near):
    tokens, shard = mine.shape
    features = cot_own.shape[1]
    size = 896 if shard % 896 == 0 else shard

    def columns(array):
        return pl.BlockSpec((array.shape[0], size), lambda i: (0, i))

    def whole(array):
        return pl.BlockSpec(array.shape, lambda i: (0, 0))

    return pl.pallas_call(
        functools.partial(weight_grad_kernel, 0.25),
        grid=(shard // size,),
        in_specs=[columns(x) for x in (mine, far, near, both)]
        + [whole(x) for x in (cot_own, cot_far, cot_near)],
        out_specs=pl.BlockSpec((size, features), lambda i: (i, 0)),
        out_shape=jax.ShapeDtypeStruct((shard, features), jnp.float32),
        compiler_params=pltpu.CompilerParams(vmem_limit_bytes=24 * MIB),
        cost_estimate=NO_COST,
        name="weight_grad",
    )(mine, far, near, both, cot_own, cot_far, cot_near)


def gradient_factors(gate_pre, up_pre):
    tok_rows = gate_pre.shape[0] // lax.axis_size("col")
    offset = lax.axis_index("col") * tok_rows
    gate_rows = lax.dynamic_slice_in_dim(gate_pre, offset, tok_rows, 0).astype(jnp.float32)
    up_rows = lax.dynamic_slice_in_dim(up_pre, offset, tok_rows, 0).astype(jnp.float32)
    sigmoid_rows = jax.nn.sigmoid(gate_rows)
    return (
        up_rows * sigmoid_rows * (1.0 + gate_rows * (1.0 - sigmoid_rows)),
        gate_rows * sigmoid_rows,
    )


def body_line(gate_pre, up_pre, down_weight, cotangent):
    tokens = gate_pre.shape[0]
    cot_other = lax.ppermute(cotangent, "row", SWAP)
    cot_beside = lax.ppermute(cotangent, "dp", FAR)
    hidden_far, low = hidden_far_and_weight(gate_pre, up_pre, down_weight)

    cot_full, ends, middle, second, third, mine = hidden_grad_parts(
        after(cotangent, cot_beside), cot_other, low, down_weight
    )
    from_end = lax.ppermute(ends, "col", ENDS)
    from_middle = lax.ppermute(middle, "col", MIDDLE)
    from_second = lax.ppermute(second, "col", ROUND_TWO)
    far = lax.ppermute(after(hidden_far, mine), "dp", FAR)

    cot_across = lax.ppermute(after(cot_beside, mine), "row", SWAP)
    hidden_near, hidden_mine, keep, send, gate_factor, up_factor = mixed_and_factors(
        gate_pre, up_pre, down_weight, after(hidden_far, cot_across)
    )
    place = lax.axis_index("col")
    transit = jnp.where((place == 1) | (place == 2), from_end, jnp.zeros_like(from_end))
    forward = (
        after(third, from_middle, keep).astype(jnp.float32) + transit.astype(jnp.float32)
    ).astype(jnp.bfloat16)
    from_third = lax.ppermute(forward, "col", ROUND_THREE)

    top = lax.axis_index("row") == 0
    cot_far = jnp.concatenate(
        [jnp.where(top, cot_beside, cot_across), jnp.where(top, cot_across, cot_beside)], axis=0
    )
    cot_near = lax.ppermute(jnp.concatenate([cot_full, cot_far], axis=0), "dp", NEAR)
    near = lax.ppermute(after(hidden_near, forward), "dp", NEAR)
    mixed = (after(keep, forward) + lax.ppermute(after(send, forward), "row", SWAP)).astype(jnp.bfloat16)
    both = lax.ppermute(far[:tokens], "dp", NEAR)
    weight_grad = weight_grad_shard(hidden_mine, far, near, both, cot_full, cot_far, cot_near)

    so_far = (
        mine.astype(jnp.float32) + from_middle.astype(jnp.float32) + from_second.astype(jnp.float32)
    )
    so_far = lax.optimization_barrier((so_far, weight_grad))[0]
    hidden_share = so_far + after(from_third, weight_grad).astype(jnp.float32)
    gate_grad = (hidden_share * gate_factor).astype(jnp.bfloat16)
    up_grad = (hidden_share * up_factor).astype(jnp.bfloat16)
    return (mixed, gate_grad, up_grad, weight_grad)


def body_general(gate_pre, up_pre, down_weight, cotangent):
    hidden = silu_product(gate_pre, up_pre)
    cot_full = lax.all_gather(cotangent, "row", axis=0, tiled=True)
    hidden_share = lax.psum_scatter(
        lax.dot_general(
            cot_full, down_weight, (((1,), (1,)), ((), ())), preferred_element_type=jnp.float32
        ).astype(jnp.bfloat16),
        "col",
        scatter_dimension=0,
        tiled=True,
    ).astype(jnp.float32)
    mixed = lax.psum_scatter(
        jnp.dot(hidden, down_weight, preferred_element_type=jnp.float32),
        "row",
        scatter_dimension=0,
        tiled=True,
    ).astype(jnp.bfloat16)
    hidden_all = lax.all_to_all(hidden, "dp", split_axis=1, concat_axis=0, tiled=True)
    cot_all = lax.all_gather(cot_full, "dp", axis=0, tiled=True)
    weight_grad = lax.dot_general(
        hidden_all, cot_all, (((0,), (0,)), ((), ())), preferred_element_type=jnp.float32
    ) / jnp.float32(lax.axis_size("dp"))
    gate_factor, up_factor = gradient_factors(gate_pre, up_pre)
    gate_grad = (hidden_share * gate_factor).astype(jnp.bfloat16)
    up_grad = (hidden_share * up_factor).astype(jnp.bfloat16)
    return (mixed, gate_grad, up_grad, weight_grad)


def solution(mesh):
    sizes = (mesh.shape["dp"], mesh.shape["row"], mesh.shape["col"])
    placed = (P("dp", "row"), P("dp", "row"), P("row", "col"), P(("dp", "row"), "col"))
    return jax.shard_map(
        body_line if sizes == (4, 2, 4) else body_general,
        mesh=mesh,
        in_specs=placed,
        out_specs=(
            P(("dp", "row"), "col"),
            P(("dp", "col"), "row"),
            P(("dp", "col"), "row"),
            P(("row", "dp"), "col"),
        ),
        check_vma=False,
    )
```

time: 301 us -> 52.2 us (0.17)
  waiting for transfers between devices: 224 us -> 12.1 us
  matrix products: 34.9 us -> 0 us
  Pallas kernels: 0 us -> 21.6 us
  other arithmetic: 21.4 us -> 3.09 us
  starting transfers between devices: 0.12 us -> 14.4 us
  between operations: 13.8 us -> 0.76 us
  blocking collectives: 7.09 us -> 0 us
    reduce_scatter x3 -> x0, waiting for transfers between devices: 224 us -> none  [the longest x1 207 us: body(): lax.psum_scatter(lax.dot_general(hidden, cot_full, (((0,), (0,)), ((), ()...]
    dot_general x3 -> x0, matrix products: 34.9 us -> none  [the longest x1 13.6 us: body(): lax.dot_general(hidden, cot_full, (((0,), (0,)), ((), ())), preferred_ele...]
    pallas_call x0 -> x4, Pallas kernels: none -> 21.6 us  [the longest x1 7.73 us: mixed_and_factors(): pl.pallas_call(mixed_kernel, in_specs=[HBM] * 3 + [VMEM], out_specs=[VMEM...]
    ppermute x0 -> x12, starting transfers between devices: none -> 14.4 us  [the longest x1 4.44 us: body_line(): from_end = lax.ppermute(ends, 'col', ENDS)]
    ppermute x0 -> x12, waiting for transfers between devices: none -> 12.1 us  [the longest x1 5.94 us: body_line(): far = lax.ppermute(after(hidden_far, mine), 'dp', FAR)]
    div x1 -> x0, other arithmetic: 7.78 us -> none  [body(): weight_grad = grad_total / jnp.float32(replicas)]
    convert_element_type x4 -> x3, other arithmetic: 9.43 us -> 1.89 us  [the longest x1 1.07 us: body_line(): up_grad = (hidden_share * up_factor).astype(jnp.bfloat16)]
    all_gather x1 -> x0, blocking collectives: 7.09 us -> none  [body(): cot_full = lax.all_gather(cotangent, 'row', axis=0, tiled=True)]
  transfers between devices with their start and end apart: 3 -> 12, of which waited for: 2 -> 6; matrix products, arithmetic and copies ran while one was open for 13% -> 4% of each run, Pallas kernels for 0% -> 31%
where the time goes in v2:
time: 52.2 us; the launch traced here: 52 us
  Pallas kernels  21.6 us (41%)
  starting transfers between devices  14.4 us (28%)
  waiting for transfers between devices  12.1 us (23%)
  other arithmetic  3.09 us (6%)
  between operations  0.76 us (1%)
    pallas_call x1, Pallas kernels, mixed_and_factors(): pl.pallas_call(mixed_kernel, in_specs=[HBM] * 3 + [VMEM], out_specs=[VMEM...  7.73 us
    ppermute x1, waiting for transfers between devices, body_line(): far = lax.ppermute(after(hidden_far, mine), 'dp', FAR)  5.94 us
    pallas_call x1, Pallas kernels, hidden_grad_parts(): pl.pallas_call(hidden_grad_kernel, in_specs=[VMEM, VMEM, VMEM, HBM], out_...  5.74 us
    ppermute x1, starting transfers between devices, body_line(): from_end = lax.ppermute(ends, 'col', ENDS)  4.44 us
    pallas_call x1, Pallas kernels, weight_grad_shard(): pl.pallas_call(functools.partial(weight_grad_kernel, 0.25), grid=(shard /...  4.41 us
    pallas_call x1, Pallas kernels, hidden_far_and_weight(): pl.pallas_call(first_kernel, in_specs=[HBM] * 3, out_specs=[VMEM] * 2, ou...  3.74 us
    ppermute x1, starting transfers between devices, body_line(): cot_beside = lax.ppermute(cotangent, 'dp', FAR)  3.03 us
    ppermute x1, waiting for transfers between devices, body_line(): from_third = lax.ppermute(forward, 'col', ROUND_THREE)  2.54 us
  transfers between devices with their start and end apart: 12, of which 6 were waited for; matrix products, arithmetic and copies ran while one was open for 4% of the time, Pallas kernels for 31%

profile of v2, /device:TPU:0, one launch (start us, length us, event | category | flops | bytes accessed | tf_op | source)
XLA Modules:
  0.0 52.0 jit_solution(17752980534935037230)
XLA Ops:
  0.6 0.0 copy-start
  0.6 3.0 %collective-permute-start = (bf16[64,1024]{1,0:T(8,128)(2,1)}, bf16[64,1024]{1,0:T(8,128)(2,1)}, u32[]{:S(2)}, u32[]{:S(2)}) collective-permute-start(bf16[64,1024]{1,0:T(8,128)(2,1)} %own_ref), channel_id=1, source_target_pairs={{0,16},{8,24},{16,0},{24,8},{1,17},{9,25},{17,1},{25,9},{2,18},{10... | collective-permute-start | bytes 393224 | tf_op jit(solution)/shard_map/ppermute | solution.py:303
  3.7 1.5 %collective-permute-start.1 = (bf16[64,1024]{1,0:T(8,128)(2,1)}, bf16[64,1024]{1,0:T(8,128)(2,1)S(1)}, u32[]{:S(2)}, u32[]{:S(2)}) collective-permute-start(bf16[64,1024]{1,0:T(8,128)(2,1)} %own_ref), channel_id=1, source_target_pairs={{0,4},{4,0},{1,5},{5,1},{2,6},{6,2},{3,7},{7,3},{8,12},{12,8},{9,1... | collective-permute-start | bytes 393224 | tf_op jit(solution)/shard_map/ppermute | solution.py:302
  5.2 3.7 %hidden_far.1 = (bf16[256,1792]{1,0:T(8,128)(2,1)S(1)}, bf16[3584,1024]{1,0:T(8,128)(2,1)S(1)}) custom-call(bf16[128,7168]{1,0:T(8,128)(2,1)} %gate_hbm.3, bf16[128,7168]{1,0:T(8,128)(2,1)} %up_hbm.3, bf16[7168,1024]{1,0:T(8,128)(2,1)} %weight_hbm.5), custom_call_target="tpu_custom_call" | custom-call | tf_op jit(solution)/shard_map/hidden_far/pallas_call | solution.py:80
  8.9 0.0 collective-permute-done
  8.9 0.0 collective-permute-done.1.other_ref
  8.9 0.0 copy-done
  8.9 5.7 %hidden_grad.1 = (bf16[128,1024]{1,0:T(8,128)(2,1)S(1)}, bf16[32,7168]{1,0:T(8,128)(2,1)S(1)}, bf16[32,7168]{1,0:T(8,128)(2,1)S(1)}, bf16[32,7168]{1,0:T(8,128)(...) custom-call(bf16[64,1024]{1,0:T(8,128)(2,1)S(1)} %copy-done, ...), custom_call_target="tpu_custom_call" | custom-call | tf_op jit(solution)/shard_map/hidden_grad/pallas_call | solution.py:140
  14.7 1.5 %collective-permute-start.2 = (bf16[64,1024]{1,0:T(8,128)(2,1)}, bf16[64,1024]{1,0:T(8,128)(2,1)}, u32[]{:S(2)}, u32[]{:S(2)}) collective-permute-start(bf16[64,1024]{1,0:T(8,128)(2,1)} %collective-permute-done), channel_id=1, source_target_pairs={{0,4},{4,0},{1,5},{5,1},{2,6},{6,2},{3,7},{7,3},{8,12},{12,8},{9,1... | collective-permute-start | bytes 393224 | tf_op jit(solution)/shard_map/ppermute | solution.py:314
  16.2 0.7 %collective-permute-start.3 = (bf16[32,7168]{1,0:T(8,128)(2,1)S(1)}, bf16[32,7168]{1,0:T(8,128)(2,1)S(1)}, u32[]{:S(2)}, u32[]{:S(2)}) collective-permute-start(bf16[32,7168]{1,0:T(8,128)(2,1)S(1)} %get-tuple-element.36), channel_id=1, source_target_pairs={{1,2},{2,1},{5,6},{6,5},{9,10},{10,9},{13,14},{14,13},{17,18},{18,... | collective-permute-start | bytes 1376264 | tf_op jit(solution)/shard_map/ppermute | solution.py:310
  16.8 4.4 %collective-permute-start.4 = (bf16[32,7168]{1,0:T(8,128)(2,1)S(1)}, bf16[32,7168]{1,0:T(8,128)(2,1)S(1)}, u32[]{:S(2)}, u32[]{:S(2)}) collective-permute-start(bf16[32,7168]{1,0:T(8,128)(2,1)S(1)} %get-tuple-element.38), channel_id=1, source_target_pairs={{0,1},{1,0},{2,3},{3,2},{4,5},{5,4},{6,7},{7,6},{8,9},{9,8},{10,11... | collective-permute-start | bytes 1376264 | tf_op jit(solution)/shard_map/ppermute | solution.py:309
  21.3 0.0 collective-permute-start.6
  21.3 0.5 collective-permute-start.7
  21.8 0.0 collective-permute-done.2
  21.8 1.0 %broadcast_select_fusion.1 = (bf16[64,1024]{1,0:T(8,128)(2,1)S(1)}, bf16[64,1024]{1,0:T(8,128)(2,1)S(1)}) fusion(bf16[64,1024]{1,0:T(8,128)(2,1)} %collective-permute-done, bf16[64,1024]{1,0:T(8,128)(2,1)} %collective-permute-done.2, pred[]{:T(512)S(6)} %eq.11), kind=kLoop, calls=%fused_computation.9 | loop fusion | flops 131072 | bytes 524289 | tf_op jit(solution)/shard_map/jit(_where)/select_n | solution.py:327
  22.8 0.1 collective-permute-start.10
  22.9 7.7 %mixed.1 = (bf16[128,1792]{1,0:T(8,128)(2,1)S(1)}, bf16[128,1792]{1,0:T(8,128)(2,1)S(1)}, f32[64,1024]{1,0:T(8,128)S(1)}, f32[64,1024]{1,0:T(8,128)S(1)}, f32[32...) custom-call(bf16[128,7168]{1,0:T(8,128)(2,1)} %gate_hbm.3, bf16[128,7168]{1,0:T(8,128)(2,1)} %up_hbm.3, ...), custom_call_target="tpu_custom_call" | custom-call | tf_op jit(solution)/shard_map/mixed/pallas_call | solution.py:232
  30.7 0.0 collective-permute-done.3
  30.7 2.0 %collective-permute-done.4 = bf16[32,7168]{1,0:T(8,128)(2,1)S(1)} collective-permute-done((bf16[32,7168]{1,0:T(8,128)(2,1)S(1)}, bf16[32,7168]{1,0:T(8,128)(2,1)S(1)}, u32[]{:S(2)}, u32[]{:S(2)}) %collective-permute-start.4) | collective-permute-done | bytes 458784 | tf_op jit(solution)/shard_map/ppermute | solution.py:309
  32.7 0.1 add_convert_fusion
  32.9 2.1 %collective-permute-start.11 = (bf16[32,7168]{1,0:T(8,128)(2,1)S(1)}, bf16[32,7168]{1,0:T(8,128)(2,1)S(1)}, u32[]{:S(2)}, u32[]{:S(2)}) collective-permute-start(bf16[32,7168]{1,0:T(8,128)(2,1)S(1)} %add_convert_fusion), channel_id=1, source_target_pairs={{0,1},{1,3},{3,2},{2,0},{4,5},{5,7},{7,6},{6,4},{8,9},{9,11},{11,1... | collective-permute-start | bytes 1376264 | tf_op jit(solution)/shard_map/ppermute | solution.py:323
  34.9 0.6 %collective-permute-start.5 = (f32[64,1024]{1,0:T(8,128)S(1)}, f32[64,1024]{1,0:T(8,128)S(1)}, u32[]{:S(2)}, u32[]{:S(2)}) collective-permute-start(f32[64,1024]{1,0:T(8,128)S(1)} %get-tuple-element.41), channel_id=1, source_target_pairs={{0,4},{4,0},{1,5},{5,1},{2,6},{6,2},{3,7},{7,3},{8,12},{12,8},{9,1... | collective-permute-start | bytes 786440 | tf_op jit(solution)/shard_map/ppermute | solution.py:331
  35.6 5.9 %collective-permute-done.7.far = bf16[256,1792]{1,0:T(8,128)(2,1)S(1)} collective-permute-done((bf16[256,1792]{1,0:T(8,128)(2,1)S(1)}, bf16[256,1792]{1,0:T(8,128)(2,1)S(1)}, u32[]{:S(2)}, u32[]{:S(2)}) %collective-permute-start.7) | collective-permute-done | bytes 917536 | tf_op jit(solution)/shard_map/ppermute | solution.py:312
  41.5 0.0 collective-permute-start.8
  41.5 0.6 %collective-permute-done.6 = bf16[32,7168]{1,0:T(8,128)(2,1)S(1)} collective-permute-done((bf16[32,7168]{1,0:T(8,128)(2,1)S(1)}, bf16[32,7168]{1,0:T(8,128)(2,1)S(1)}, u32[]{:S(2)}, u32[]{:S(2)}) %collective-permute-start.6) | collective-permute-done | bytes 458784 | tf_op jit(solution)/shard_map/ppermute | solution.py:311
  42.1 0.0 collective-permute-start.9
  42.1 0.2 convert_add_fusion.1
  42.3 0.0 collective-permute-done.5
  42.3 0.7 %add_convert_fusion.1 = bf16[64,1024]{1,0:T(8,128)(2,1)} fusion(f32[64,1024]{1,0:T(8,128)S(1)} %get-tuple-element.39, f32[64,1024]{1,0:T(8,128)S(1)} %collective-permute-done.5), kind=kLoop, calls=%fused_computation.7 | loop fusion | flops 131072 | bytes 655360 | tf_op jit(solution)/shard_map/convert_element_type | solution.py:331
  43.0 0.0 collective-permute-done.10.cot_near
  43.0 0.3 collective-permute-done.8.near
  43.3 0.7 %collective-permute-done.9.both = bf16[128,1792]{1,0:T(8,128)(2,1)S(1)} collective-permute-done((bf16[128,1792]{1,0:T(8,128)(2,1)S(1)}, bf16[128,1792]{1,0:T(8,128)(2,1)S(1)}, u32[]{:S(2)}, u32[]{:S(2)}) %collective-permute-start.9) | collective-permute-done | bytes 458784 | tf_op jit(solution)/shard_map/ppermute | solution.py:332
  44.0 4.4 %weight_grad.1 = f32[1792,1024]{1,0:T(8,128)} custom-call(bf16[128,1792]{1,0:T(8,128)(2,1)S(1)} %get-tuple-element.43.mine, bf16[256,1792]{1,0:T(8,128)(2,1)S(1)} %collective-permute-done.7.far, bf16[128,1792]{1,0:T(8,128)(2,1)S(1)} %collective-permute-done.8.near, bf16[128,1792]{1,0:T(8,128)(2,1)S(1)} %collective-permute-done.9.both, ...), custom_call_target="tpu_custom_call" | custom-call | tf_op jit(solution)/shard_map/weight_grad/pallas_call | solution.py:275
  48.4 2.5 %collective-permute-done.11 = bf16[32,7168]{1,0:T(8,128)(2,1)S(1)} collective-permute-done((bf16[32,7168]{1,0:T(8,128)(2,1)S(1)}, bf16[32,7168]{1,0:T(8,128)(2,1)S(1)}, u32[]{:S(2)}, u32[]{:S(2)}) %collective-permute-start.11) | collective-permute-done | bytes 458784 | tf_op jit(solution)/shard_map/ppermute | solution.py:323
  50.9 1.1 %multiply_convert_fusion = (bf16[32,7168]{1,0:T(8,128)(2,1)}, bf16[32,7168]{1,0:T(8,128)(2,1)}) fusion(f32[32,7168]{1,0:T(8,128)S(1)} %get-tuple-element.51, f32[32,7168]{1,0:T(8,128)S(1)} %convert_add_fusion.1, bf16[32,7168]{1,0:T(8,128)(2,1)S(1)} %collective-permute-done.11, f32[32,7168]{1,0:T(8,128)S(1)} %get-tuple-element.50), kind=kLoop, calls=%fused_computation | loop fusion | flops 1376256 | bytes 4128768 | tf_op jit(solution)/shard_map/convert_element_type | solution.py:341
  (3 shorter events, 0.1 us)
Async XLA Ops:
  0.6 8.3 %copy-start = (bf16[64,1024]{1,0:T(8,128)(2,1)S(1)}, bf16[64,1024]{1,0:T(8,128)(2,1)}, u32[]{:S(2)}) copy-start(bf16[64,1024]{1,0:T(8,128)(2,1)} %own_ref) | copy-start | bytes 393220
  0.6 8.3 %collective-permute-start = (bf16[64,1024]{1,0:T(8,128)(2,1)}, bf16[64,1024]{1,0:T(8,128)(2,1)}, u32[]{:S(2)}, u32[]{:S(2)}) collective-permute-start(bf16[64,1024]{1,0:T(8,128)(2,1)} %own_ref), channel_id=1, source_target_pairs={{0,16},{8,24},{16,0},{24,8},{1,17},{9,25},{17,1},{25,9},{2,18},{10... | collective-permute-start | bytes 393224 | tf_op jit(solution)/shard_map/ppermute | solution.py:303
  3.7 5.3 %collective-permute-start.1 = (bf16[64,1024]{1,0:T(8,128)(2,1)}, bf16[64,1024]{1,0:T(8,128)(2,1)S(1)}, u32[]{:S(2)}, u32[]{:S(2)}) collective-permute-start(bf16[64,1024]{1,0:T(8,128)(2,1)} %own_ref), channel_id=1, source_target_pairs={{0,4},{4,0},{1,5},{5,1},{2,6},{6,2},{3,7},{7,3},{8,12},{12,8},{9,1... | collective-permute-start | bytes 393224 | tf_op jit(solution)/shard_map/ppermute | solution.py:302
  14.7 7.1 %collective-permute-start.2 = (bf16[64,1024]{1,0:T(8,128)(2,1)}, bf16[64,1024]{1,0:T(8,128)(2,1)}, u32[]{:S(2)}, u32[]{:S(2)}) collective-permute-start(bf16[64,1024]{1,0:T(8,128)(2,1)} %collective-permute-done), channel_id=1, source_target_pairs={{0,4},{4,0},{1,5},{5,1},{2,6},{6,2},{3,7},{7,3},{8,12},{12,8},{9,1... | collective-permute-start | bytes 393224 | tf_op jit(solution)/shard_map/ppermute | solution.py:314
  16.2 14.5 %collective-permute-start.3 = (bf16[32,7168]{1,0:T(8,128)(2,1)S(1)}, bf16[32,7168]{1,0:T(8,128)(2,1)S(1)}, u32[]{:S(2)}, u32[]{:S(2)}) collective-permute-start(bf16[32,7168]{1,0:T(8,128)(2,1)S(1)} %get-tuple-element.36), channel_id=1, source_target_pairs={{1,2},{2,1},{5,6},{6,5},{9,10},{10,9},{13,14},{14,13},{17,18},{18,... | collective-permute-start | bytes 1376264 | tf_op jit(solution)/shard_map/ppermute | solution.py:310
  16.8 15.9 %collective-permute-start.4 = (bf16[32,7168]{1,0:T(8,128)(2,1)S(1)}, bf16[32,7168]{1,0:T(8,128)(2,1)S(1)}, u32[]{:S(2)}, u32[]{:S(2)}) collective-permute-start(bf16[32,7168]{1,0:T(8,128)(2,1)S(1)} %get-tuple-element.38), channel_id=1, source_target_pairs={{0,1},{1,0},{2,3},{3,2},{4,5},{5,4},{6,7},{7,6},{8,9},{9,8},{10,11... | collective-permute-start | bytes 1376264 | tf_op jit(solution)/shard_map/ppermute | solution.py:309
  21.3 20.9 %collective-permute-start.6 = (bf16[32,7168]{1,0:T(8,128)(2,1)S(1)}, bf16[32,7168]{1,0:T(8,128)(2,1)S(1)}, u32[]{:S(2)}, u32[]{:S(2)}) collective-permute-start(bf16[32,7168]{1,0:T(8,128)(2,1)S(1)} %get-tuple-element.42), channel_id=1, source_target_pairs={{0,2},{2,3},{3,1},{1,0},{4,6},{6,7},{7,5},{5,4},{8,10},{10,11},{11... | collective-permute-start | bytes 1376264 | tf_op jit(solution)/shard_map/ppermute | solution.py:311
  21.3 20.2 %collective-permute-start.7 = (bf16[256,1792]{1,0:T(8,128)(2,1)S(1)}, bf16[256,1792]{1,0:T(8,128)(2,1)S(1)}, u32[]{:S(2)}, u32[]{:S(2)}) collective-permute-start(bf16[256,1792]{1,0:T(8,128)(2,1)S(1)} %get-tuple-element.44.far_ref), channel_id=1, source_target_pairs={{0,16},{8,24},{16,0},{24,8},{1,17},{9,25},{17,1},{25,9},{2,18},{10... | collective-permute-start | bytes 2752520 | tf_op jit(solution)/shard_map/ppermute | solution.py:312
  22.8 20.1 %collective-permute-start.10 = (bf16[256,1024]{1,0:T(8,128)(2,1)S(1)}, bf16[256,1024]{1,0:T(8,128)(2,1)S(1)}, u32[]{:S(2)}, u32[]{:S(2)}) collective-permute-start(bf16[256,1024]{1,0:T(8,128)(2,1)S(1)} %pad_maximum_fusion), channel_id=1, source_target_pairs={{0,8},{8,0},{16,24},{24,16},{1,9},{9,1},{17,25},{25,17},{2,10},{10... | collective-permute-start | bytes 1572872 | tf_op jit(solution)/shard_map/ppermute | solution.py:329
  32.9 18.1 %collective-permute-start.11 = (bf16[32,7168]{1,0:T(8,128)(2,1)S(1)}, bf16[32,7168]{1,0:T(8,128)(2,1)S(1)}, u32[]{:S(2)}, u32[]{:S(2)}) collective-permute-start(bf16[32,7168]{1,0:T(8,128)(2,1)S(1)} %add_convert_fusion), channel_id=1, source_target_pairs={{0,1},{1,3},{3,2},{2,0},{4,5},{5,7},{7,6},{6,4},{8,9},{9,11},{11,1... | collective-permute-start | bytes 1376264 | tf_op jit(solution)/shard_map/ppermute | solution.py:323
  34.9 7.4 %collective-permute-start.5 = (f32[64,1024]{1,0:T(8,128)S(1)}, f32[64,1024]{1,0:T(8,128)S(1)}, u32[]{:S(2)}, u32[]{:S(2)}) collective-permute-start(f32[64,1024]{1,0:T(8,128)S(1)} %get-tuple-element.41), channel_id=1, source_target_pairs={{0,4},{4,0},{1,5},{5,1},{2,6},{6,2},{3,7},{7,3},{8,12},{12,8},{9,1... | collective-permute-start | bytes 786440 | tf_op jit(solution)/shard_map/ppermute | solution.py:331
  41.5 1.8 %collective-permute-start.8 = (bf16[128,1792]{1,0:T(8,128)(2,1)S(1)}, bf16[128,1792]{1,0:T(8,128)(2,1)S(1)}, u32[]{:S(2)}, u32[]{:S(2)}) collective-permute-start(bf16[128,1792]{1,0:T(8,128)(2,1)S(1)} %get-tuple-element.46), channel_id=1, source_target_pairs={{0,8},{8,0},{16,24},{24,16},{1,9},{9,1},{17,25},{25,17},{2,10},{10... | collective-permute-start | bytes 1376264 | tf_op jit(solution)/shard_map/ppermute | solution.py:330
  42.1 1.8 %collective-permute-start.9 = (bf16[128,1792]{1,0:T(8,128)(2,1)S(1)}, bf16[128,1792]{1,0:T(8,128)(2,1)S(1)}, u32[]{:S(2)}, u32[]{:S(2)}) collective-permute-start(bf16[128,1792]{1,0:T(8,128)(2,1)S(1)} %slice.4), channel_id=1, source_target_pairs={{0,8},{8,0},{16,24},{24,16},{1,9},{9,1},{17,25},{25,17},{2,10},{10... | collective-permute-start | bytes 1376264 | tf_op jit(solution)/shard_map/ppermute | solution.py:332

commit v3 on v2

--- a/solution.py
+++ b/solution.py
@@ -19,7 +19,7 @@
 VMEM = pl.BlockSpec(memory_space=pltpu.VMEM)
 HBM = pl.BlockSpec(memory_space=pltpu.HBM)
 MIB = 2**20
-CHUNK = 896
+CHUNK = 256
 NO_COST = pl.CostEstimate(flops=0, bytes_accessed=0, transcendentals=0)
 
 
@@ -33,6 +33,13 @@
 
 def in_vmem(array):
     return pltpu.with_memory_space_constraint(array, pltpu.VMEM)
+
+
+def settled(array):
+    top = lax.axis_index("row") == 0
+    turned = lax.optimization_barrier(-array)
+    turned = lax.optimization_barrier(jnp.where(top, -turned, turned))
+    return lax.optimization_barrier(jnp.where(top, turned, -turned))
 
 
 def silu_product(gate, up):
@@ -99,8 +106,16 @@
     own_ref, other_ref, low_ref, weight_hbm, full_ref, ends, middle, second, third, mine, ordered_ref, high_ref, sem
 ):
     units = low_ref.shape[0]
-    load = pltpu.make_async_copy(weight_hbm.at[units:], high_ref, sem.at[0])
-    load.start()
+    quarter = units // 2
+
+    def load(i):
+        rows = pl.ds(i * quarter, quarter)
+        return pltpu.make_async_copy(
+            weight_hbm.at[pl.ds(units + i * quarter, quarter)], high_ref.at[rows], sem.at[i]
+        )
+
+    load(0).start()
+    load(1).start()
     half = own_ref.shape[0]
     tokens = half // 2
     top = lax.axis_index("row") == 0
@@ -113,11 +128,11 @@
             block = jnp.where(place == z, jnp.int32(SEND_ORDER[z][i]), block)
         start = pl.multiple_of(block * tokens, tokens)
         ordered_ref[i * tokens : (i + 1) * tokens] = full_ref[pl.ds(start, tokens)]
-    size = CHUNK if units % CHUNK == 0 else units
+    size = CHUNK if quarter % CHUNK == 0 else quarter
     for base, weight_ref in ((0, low_ref), (units, high_ref)):
-        if base:
-            load.wait()
         for start in range(0, units, size):
+            if base and start % quarter == 0:
+                load(start // quarter).wait()
             product = lax.dot_general(
                 weight_ref[start : start + size],
                 ordered_ref[...],
@@ -145,7 +160,7 @@
         scratch_shapes=[
             pltpu.VMEM((2 * half, depth), jnp.bfloat16),
             pltpu.VMEM((units, depth), jnp.bfloat16),
-            pltpu.SemaphoreType.DMA((1,)),
+            pltpu.SemaphoreType.DMA((2,)),
         ],
         compiler_params=pltpu.CompilerParams(vmem_limit_bytes=24 * MIB),
         cost_estimate=NO_COST,
@@ -300,20 +315,19 @@
 def body_line(gate_pre, up_pre, down_weight, cotangent):
     tokens = gate_pre.shape[0]
     cot_other = lax.ppermute(cotangent, "row", SWAP)
-    cot_beside = lax.ppermute(cotangent, "dp", FAR)
     hidden_far, low = hidden_far_and_weight(gate_pre, up_pre, down_weight)
 
     cot_full, ends, middle, second, third, mine = hidden_grad_parts(
-        after(cotangent, cot_beside), cot_other, low, down_weight
+        cotangent, cot_other, low, down_weight
     )
     from_end = lax.ppermute(ends, "col", ENDS)
     from_middle = lax.ppermute(middle, "col", MIDDLE)
     from_second = lax.ppermute(second, "col", ROUND_TWO)
     far = lax.ppermute(after(hidden_far, mine), "dp", FAR)
 
-    cot_across = lax.ppermute(after(cot_beside, mine), "row", SWAP)
+    cot_far = lax.ppermute(after(cot_full, mine), "dp", FAR)
     hidden_near, hidden_mine, keep, send, gate_factor, up_factor = mixed_and_factors(
-        gate_pre, up_pre, down_weight, after(hidden_far, cot_across)
+        gate_pre, up_pre, down_weight, after(hidden_far, cot_far)
     )
     place = lax.axis_index("col")
     transit = jnp.where((place == 1) | (place == 2), from_end, jnp.zeros_like(from_end))
@@ -322,10 +336,7 @@
     ).astype(jnp.bfloat16)
     from_third = lax.ppermute(forward, "col", ROUND_THREE)
 
-    top = lax.axis_index("row") == 0
-    cot_far = jnp.concatenate(
-        [jnp.where(top, cot_beside, cot_across), jnp.where(top, cot_across, cot_beside)], axis=0
-    )
+    cot_far = settled(cot_far)
     cot_near = lax.ppermute(jnp.concatenate([cot_full, cot_far], axis=0), "dp", NEAR)
     near = lax.ppermute(after(hidden_near, forward), "dp", NEAR)
     mixed = (after(keep, forward) + lax.ppermute(after(send, forward), "row", SWAP)).astype(jnp.bfloat16)

time: 52.2 us -> 50.7 us (0.971)
  waiting for transfers between devices: 12.1 us -> 11.2 us
  Pallas kernels: 21.6 us -> 20.8 us
    ppermute x2 -> x1, starting transfers between devices: 4.49 us -> 1.77 us  [body_line(): cot_far = lax.ppermute(after(cot_full, mine), 'dp', FAR)]
    ppermute x1, starting transfers between devices: 1.49 us -> 3 us  [body_line(): cot_other = lax.ppermute(cotangent, 'row', SWAP)]
    neg x0 -> x1, other arithmetic: none -> 1 us  [settled(): turned = lax.optimization_barrier(-array)]
    select_n x1 -> x2, other arithmetic: 0.99 us -> 0.05 us  [the longest x1 0.02 us: settled(): return lax.optimization_barrier(jnp.where(top, turned, -turned))]
    ppermute x1, starting transfers between devices: 0.63 us -> 1.49 us  [body_line(): lax.ppermute(after(send, forward), 'row', SWAP)]
    pallas_call x1, Pallas kernels: 5.74 us -> 4.9 us  [hidden_grad_parts(): pl.pallas_call(hidden_grad_kernel, in_specs=[VMEM, VMEM, VMEM, HBM], out_...]
    ppermute x1, waiting for transfers between devices: 0.59 us -> 0.01 us  [body_line(): from_second = lax.ppermute(second, 'col', ROUND_TWO)]
    ppermute x1, waiting for transfers between devices: 2.03 us -> 1.45 us  [body_line(): from_end = lax.ppermute(ends, 'col', ENDS)]
  transfers between devices with their start and end apart: 12 -> 11, of which waited for: 6 -> 6; matrix products, arithmetic and copies ran while one was open for 4% -> 4% of each run, Pallas kernels for 31% -> 31%
where the time goes in v3:
time: 50.7 us; the launch traced here: 50.5 us
  Pallas kernels  20.8 us (41%)
  starting transfers between devices  14.6 us (29%)
  waiting for transfers between devices  11.2 us (22%)
  other arithmetic  3.13 us (6%)
  between operations  0.77 us (2%)
    pallas_call x1, Pallas kernels, mixed_and_factors(): pl.pallas_call(mixed_kernel, in_specs=[HBM] * 3 + [VMEM], out_specs=[VMEM...  7.73 us
    ppermute x1, waiting for transfers between devices, body_line(): far = lax.ppermute(after(hidden_far, mine), 'dp', FAR)  5.67 us
    pallas_call x1, Pallas kernels, hidden_grad_parts(): pl.pallas_call(hidden_grad_kernel, in_specs=[VMEM, VMEM, VMEM, HBM], out_...  4.9 us
    ppermute x1, starting transfers between devices, body_line(): from_end = lax.ppermute(ends, 'col', ENDS)  4.43 us
    pallas_call x1, Pallas kernels, weight_grad_shard(): pl.pallas_call(functools.partial(weight_grad_kernel, 0.25), grid=(shard /...  4.41 us
    pallas_call x1, Pallas kernels, hidden_far_and_weight(): pl.pallas_call(first_kernel, in_specs=[HBM] * 3, out_specs=[VMEM] * 2, ou...  3.74 us
    ppermute x1, starting transfers between devices, body_line(): cot_other = lax.ppermute(cotangent, 'row', SWAP)  3 us
    ppermute x1, waiting for transfers between devices, body_line(): from_third = lax.ppermute(forward, 'col', ROUND_THREE)  2.56 us
  transfers between devices with their start and end apart: 11, of which 6 were waited for; matrix products, arithmetic and copies ran while one was open for 4% of the time, Pallas kernels for 31%

profile of v3, /device:TPU:0, one launch (start us, length us, event | category | flops | bytes accessed | tf_op | source)
XLA Modules:
  0.0 50.5 jit_solution(1268109299741856968)
XLA Ops:
  0.6 0.0 copy-start
  0.6 3.0 %collective-permute-start = (bf16[64,1024]{1,0:T(8,128)(2,1)}, bf16[64,1024]{1,0:T(8,128)(2,1)S(1)}, u32[]{:S(2)}, u32[]{:S(2)}) collective-permute-start(bf16[64,1024]{1,0:T(8,128)(2,1)} %own_ref.1), channel_id=1, source_target_pairs={{0,4},{4,0},{1,5},{5,1},{2,6},{6,2},{3,7},{7,3},{8,12},{12,8},{9,1... | collective-permute-start | bytes 393224 | tf_op jit(solution)/shard_map/ppermute | solution.py:317
  3.6 3.7 %hidden_far.1 = (bf16[256,1792]{1,0:T(8,128)(2,1)S(1)}, bf16[3584,1024]{1,0:T(8,128)(2,1)S(1)}) custom-call(bf16[128,7168]{1,0:T(8,128)(2,1)} %gate_hbm.3, bf16[128,7168]{1,0:T(8,128)(2,1)} %up_hbm.3, bf16[7168,1024]{1,0:T(8,128)(2,1)} %weight_hbm.5), custom_call_target="tpu_custom_call" | custom-call | tf_op jit(solution)/shard_map/hidden_far/pallas_call | solution.py:87
  7.4 0.0 collective-permute-done.other_ref
  7.4 0.0 copy-done
  7.4 4.9 %hidden_grad.1 = (bf16[128,1024]{1,0:T(8,128)(2,1)S(1)}, bf16[32,7168]{1,0:T(8,128)(2,1)S(1)}, bf16[32,7168]{1,0:T(8,128)(2,1)S(1)}, bf16[32,7168]{1,0:T(8,128)(...) custom-call(bf16[64,1024]{1,0:T(8,128)(2,1)S(1)} %copy-done, ...), custom_call_target="tpu_custom_call" | custom-call | tf_op jit(solution)/shard_map/hidden_grad/pallas_call | solution.py:155
  12.3 1.8 %collective-permute-start.1 = (bf16[128,1024]{1,0:T(8,128)(2,1)S(1)}, bf16[128,1024]{1,0:T(8,128)(2,1)}, u32[]{:S(2)}, u32[]{:S(2)}) collective-permute-start(bf16[128,1024]{1,0:T(8,128)(2,1)S(1)} %get-tuple-element.31.cot_own), channel_id=1, source_target_pairs={{0,16},{8,24},{16,0},{24,8},{1,17},{9,25},{17,1},{25,9},{2,18},{10... | collective-permute-start | bytes 786440 | tf_op jit(solution)/shard_map/ppermute | solution.py:328
  14.1 0.7 %collective-permute-start.2 = (bf16[32,7168]{1,0:T(8,128)(2,1)S(1)}, bf16[32,7168]{1,0:T(8,128)(2,1)S(1)}, u32[]{:S(2)}, u32[]{:S(2)}) collective-permute-start(bf16[32,7168]{1,0:T(8,128)(2,1)S(1)} %get-tuple-element.35), channel_id=1, source_target_pairs={{1,2},{2,1},{5,6},{6,5},{9,10},{10,9},{13,14},{14,13},{17,18},{18,... | collective-permute-start | bytes 1376264 | tf_op jit(solution)/shard_map/ppermute | solution.py:324
  14.8 4.4 %collective-permute-start.3 = (bf16[32,7168]{1,0:T(8,128)(2,1)S(1)}, bf16[32,7168]{1,0:T(8,128)(2,1)S(1)}, u32[]{:S(2)}, u32[]{:S(2)}) collective-permute-start(bf16[32,7168]{1,0:T(8,128)(2,1)S(1)} %get-tuple-element.37), channel_id=1, source_target_pairs={{0,1},{1,0},{2,3},{3,2},{4,5},{5,4},{6,7},{7,6},{8,9},{9,8},{10,11... | collective-permute-start | bytes 1376264 | tf_op jit(solution)/shard_map/ppermute | solution.py:323
  19.2 0.0 collective-permute-start.5
  19.2 0.5 %collective-permute-start.6 = (bf16[256,1792]{1,0:T(8,128)(2,1)S(1)}, bf16[256,1792]{1,0:T(8,128)(2,1)S(1)}, u32[]{:S(2)}, u32[]{:S(2)}) collective-permute-start(bf16[256,1792]{1,0:T(8,128)(2,1)S(1)} %get-tuple-element.43.far_ref), channel_id=1, source_target_pairs={{0,16},{8,24},{16,0},{24,8},{1,17},{9,25},{17,1},{25,9},{2,18},{10... | collective-permute-start | bytes 2752520 | tf_op jit(solution)/shard_map/ppermute | solution.py:326
  19.7 0.5 %collective-permute-done.1 = bf16[128,1024]{1,0:T(8,128)(2,1)} collective-permute-done((bf16[128,1024]{1,0:T(8,128)(2,1)S(1)}, bf16[128,1024]{1,0:T(8,128)(2,1)}, u32[]{:S(2)}, u32[]{:S(2)}) %collective-permute-start.1) | collective-permute-done | bytes 262176 | tf_op jit(solution)/shard_map/ppermute | solution.py:328
  20.3 1.0 %neg.9 = bf16[128,1024]{1,0:T(8,128)(2,1)S(1)} negate(bf16[128,1024]{1,0:T(8,128)(2,1)} %collective-permute-done.1) | non-fusion elementwise | flops 131072 | bytes 524288 | tf_op jit(solution)/shard_map/neg | solution.py:40
  21.4 0.1 collective-permute-start.9
  21.4 7.7 %mixed.1 = (bf16[128,1792]{1,0:T(8,128)(2,1)S(1)}, bf16[128,1792]{1,0:T(8,128)(2,1)S(1)}, f32[64,1024]{1,0:T(8,128)S(1)}, f32[64,1024]{1,0:T(8,128)S(1)}, f32[32...) custom-call(bf16[128,7168]{1,0:T(8,128)(2,1)} %gate_hbm.3, bf16[128,7168]{1,0:T(8,128)(2,1)} %up_hbm.3, ...), custom_call_target="tpu_custom_call" | custom-call | tf_op jit(solution)/shard_map/mixed/pallas_call | solution.py:247
  29.2 0.0 collective-permute-done.2
  29.2 1.4 %collective-permute-done.3 = bf16[32,7168]{1,0:T(8,128)(2,1)S(1)} collective-permute-done((bf16[32,7168]{1,0:T(8,128)(2,1)S(1)}, bf16[32,7168]{1,0:T(8,128)(2,1)S(1)}, u32[]{:S(2)}, u32[]{:S(2)}) %collective-permute-start.3) | collective-permute-done | bytes 458784 | tf_op jit(solution)/shard_map/ppermute | solution.py:323
  30.6 0.1 add_convert_fusion
  30.8 2.1 %collective-permute-start.10 = (bf16[32,7168]{1,0:T(8,128)(2,1)S(1)}, bf16[32,7168]{1,0:T(8,128)(2,1)S(1)}, u32[]{:S(2)}, u32[]{:S(2)}) collective-permute-start(bf16[32,7168]{1,0:T(8,128)(2,1)S(1)} %add_convert_fusion), channel_id=1, source_target_pairs={{0,1},{1,3},{3,2},{2,0},{4,5},{5,7},{7,6},{6,4},{8,9},{9,11},{11,1... | collective-permute-start | bytes 1376264 | tf_op jit(solution)/shard_map/ppermute | solution.py:337
  32.9 1.5 %collective-permute-start.4 = (f32[64,1024]{1,0:T(8,128)S(1)}, f32[64,1024]{1,0:T(8,128)S(1)}, u32[]{:S(2)}, u32[]{:S(2)}) collective-permute-start(f32[64,1024]{1,0:T(8,128)S(1)} %get-tuple-element.40), channel_id=1, source_target_pairs={{0,4},{4,0},{1,5},{5,1},{2,6},{6,2},{3,7},{7,3},{8,12},{12,8},{9,1... | collective-permute-start | bytes 786440 | tf_op jit(solution)/shard_map/ppermute | solution.py:342
  34.3 5.7 %collective-permute-done.6.far = bf16[256,1792]{1,0:T(8,128)(2,1)S(1)} collective-permute-done((bf16[256,1792]{1,0:T(8,128)(2,1)S(1)}, bf16[256,1792]{1,0:T(8,128)(2,1)S(1)}, u32[]{:S(2)}, u32[]{:S(2)}) %collective-permute-start.6) | collective-permute-done | bytes 917536 | tf_op jit(solution)/shard_map/ppermute | solution.py:326
  40.0 0.0 collective-permute-start.7
  40.1 0.0 collective-permute-done.5
  40.1 0.6 %collective-permute-start.8 = (bf16[128,1792]{1,0:T(8,128)(2,1)S(1)}, bf16[128,1792]{1,0:T(8,128)(2,1)S(1)}, u32[]{:S(2)}, u32[]{:S(2)}) collective-permute-start(bf16[128,1792]{1,0:T(8,128)(2,1)S(1)} %slice.4), channel_id=1, source_target_pairs={{0,8},{8,0},{16,24},{24,16},{1,9},{9,1},{17,25},{25,17},{2,10},{10... | collective-permute-start | bytes 1376264 | tf_op jit(solution)/shard_map/ppermute | solution.py:343
  40.6 0.2 convert_add_fusion.1
  40.8 0.0 collective-permute-done.4
  40.8 0.7 %add_convert_fusion.1 = bf16[64,1024]{1,0:T(8,128)(2,1)} fusion(f32[64,1024]{1,0:T(8,128)S(1)} %get-tuple-element.38, f32[64,1024]{1,0:T(8,128)S(1)} %collective-permute-done.4), kind=kLoop, calls=%fused_computation.8 | loop fusion | flops 131072 | bytes 655360 | tf_op jit(solution)/shard_map/convert_element_type | solution.py:342
  41.5 0.0 collective-permute-done.9.cot_near
  41.5 0.3 collective-permute-done.7.near
  41.8 0.7 %collective-permute-done.8.both = bf16[128,1792]{1,0:T(8,128)(2,1)S(1)} collective-permute-done((bf16[128,1792]{1,0:T(8,128)(2,1)S(1)}, bf16[128,1792]{1,0:T(8,128)(2,1)S(1)}, u32[]{:S(2)}, u32[]{:S(2)}) %collective-permute-start.8) | collective-permute-done | bytes 458784 | tf_op jit(solution)/shard_map/ppermute | solution.py:343
  42.5 4.4 %weight_grad.1 = f32[1792,1024]{1,0:T(8,128)} custom-call(bf16[128,1792]{1,0:T(8,128)(2,1)S(1)} %get-tuple-element.42.mine, bf16[256,1792]{1,0:T(8,128)(2,1)S(1)} %collective-permute-done.6.far, bf16[128,1792]{1,0:T(8,128)(2,1)S(1)} %collective-permute-done.7.near, bf16[128,1792]{1,0:T(8,128)(2,1)S(1)} %collective-permute-done.8.both, ...), custom_call_target="tpu_custom_call" | custom-call | tf_op jit(solution)/shard_map/weight_grad/pallas_call | solution.py:290
  46.9 2.6 %collective-permute-done.10 = bf16[32,7168]{1,0:T(8,128)(2,1)S(1)} collective-permute-done((bf16[32,7168]{1,0:T(8,128)(2,1)S(1)}, bf16[32,7168]{1,0:T(8,128)(2,1)S(1)}, u32[]{:S(2)}, u32[]{:S(2)}) %collective-permute-start.10) | collective-permute-done | bytes 458784 | tf_op jit(solution)/shard_map/ppermute | solution.py:337
  49.5 1.1 %multiply_convert_fusion = (bf16[32,7168]{1,0:T(8,128)(2,1)}, bf16[32,7168]{1,0:T(8,128)(2,1)}) fusion(f32[32,7168]{1,0:T(8,128)S(1)} %get-tuple-element.49, f32[32,7168]{1,0:T(8,128)S(1)} %convert_add_fusion.1, bf16[32,7168]{1,0:T(8,128)(2,1)S(1)} %collective-permute-done.10, f32[32,7168]{1,0:T(8,128)S(1)} %get-tuple-element.48), kind=kLoop, calls=%fused_computation | loop fusion | flops 1376256 | bytes 4128768 | tf_op jit(solution)/shard_map/convert_element_type | solution.py:352
  (4 shorter events, 0.1 us)
Async XLA Ops:
  0.6 6.8 %copy-start = (bf16[64,1024]{1,0:T(8,128)(2,1)S(1)}, bf16[64,1024]{1,0:T(8,128)(2,1)}, u32[]{:S(2)}) copy-start(bf16[64,1024]{1,0:T(8,128)(2,1)} %own_ref.1) | copy-start | bytes 393220
  0.6 6.8 %collective-permute-start = (bf16[64,1024]{1,0:T(8,128)(2,1)}, bf16[64,1024]{1,0:T(8,128)(2,1)S(1)}, u32[]{:S(2)}, u32[]{:S(2)}) collective-permute-start(bf16[64,1024]{1,0:T(8,128)(2,1)} %own_ref.1), channel_id=1, source_target_pairs={{0,4},{4,0},{1,5},{5,1},{2,6},{6,2},{3,7},{7,3},{8,12},{12,8},{9,1... | collective-permute-start | bytes 393224 | tf_op jit(solution)/shard_map/ppermute | solution.py:317
  12.3 7.9 %collective-permute-start.1 = (bf16[128,1024]{1,0:T(8,128)(2,1)S(1)}, bf16[128,1024]{1,0:T(8,128)(2,1)}, u32[]{:S(2)}, u32[]{:S(2)}) collective-permute-start(bf16[128,1024]{1,0:T(8,128)(2,1)S(1)} %get-tuple-element.31.cot_own), channel_id=1, source_target_pairs={{0,16},{8,24},{16,0},{24,8},{1,17},{9,25},{17,1},{25,9},{2,18},{10... | collective-permute-start | bytes 786440 | tf_op jit(solution)/shard_map/ppermute | solution.py:328
  14.1 15.1 %collective-permute-start.2 = (bf16[32,7168]{1,0:T(8,128)(2,1)S(1)}, bf16[32,7168]{1,0:T(8,128)(2,1)S(1)}, u32[]{:S(2)}, u32[]{:S(2)}) collective-permute-start(bf16[32,7168]{1,0:T(8,128)(2,1)S(1)} %get-tuple-element.35), channel_id=1, source_target_pairs={{1,2},{2,1},{5,6},{6,5},{9,10},{10,9},{13,14},{14,13},{17,18},{18,... | collective-permute-start | bytes 1376264 | tf_op jit(solution)/shard_map/ppermute | solution.py:324
  14.8 15.9 %collective-permute-start.3 = (bf16[32,7168]{1,0:T(8,128)(2,1)S(1)}, bf16[32,7168]{1,0:T(8,128)(2,1)S(1)}, u32[]{:S(2)}, u32[]{:S(2)}) collective-permute-start(bf16[32,7168]{1,0:T(8,128)(2,1)S(1)} %get-tuple-element.37), channel_id=1, source_target_pairs={{0,1},{1,0},{2,3},{3,2},{4,5},{5,4},{6,7},{7,6},{8,9},{9,8},{10,11... | collective-permute-start | bytes 1376264 | tf_op jit(solution)/shard_map/ppermute | solution.py:323
  19.2 20.9 %collective-permute-start.5 = (bf16[32,7168]{1,0:T(8,128)(2,1)S(1)}, bf16[32,7168]{1,0:T(8,128)(2,1)S(1)}, u32[]{:S(2)}, u32[]{:S(2)}) collective-permute-start(bf16[32,7168]{1,0:T(8,128)(2,1)S(1)} %get-tuple-element.41), channel_id=1, source_target_pairs={{0,2},{2,3},{3,1},{1,0},{4,6},{6,7},{7,5},{5,4},{8,10},{10,11},{11... | collective-permute-start | bytes 1376264 | tf_op jit(solution)/shard_map/ppermute | solution.py:325
  19.2 20.8 %collective-permute-start.6 = (bf16[256,1792]{1,0:T(8,128)(2,1)S(1)}, bf16[256,1792]{1,0:T(8,128)(2,1)S(1)}, u32[]{:S(2)}, u32[]{:S(2)}) collective-permute-start(bf16[256,1792]{1,0:T(8,128)(2,1)S(1)} %get-tuple-element.43.far_ref), channel_id=1, source_target_pairs={{0,16},{8,24},{16,0},{24,8},{1,17},{9,25},{17,1},{25,9},{2,18},{10... | collective-permute-start | bytes 2752520 | tf_op jit(solution)/shard_map/ppermute | solution.py:326
  21.4 20.1 %collective-permute-start.9 = (bf16[256,1024]{1,0:T(8,128)(2,1)S(1)}, bf16[256,1024]{1,0:T(8,128)(2,1)S(1)}, u32[]{:S(2)}, u32[]{:S(2)}) collective-permute-start(bf16[256,1024]{1,0:T(8,128)(2,1)S(1)} %pad_maximum_fusion), channel_id=1, source_target_pairs={{0,8},{8,0},{16,24},{24,16},{1,9},{9,1},{17,25},{25,17},{2,10},{10... | collective-permute-start | bytes 1572872 | tf_op jit(solution)/shard_map/ppermute | solution.py:340
  30.8 18.7 %collective-permute-start.10 = (bf16[32,7168]{1,0:T(8,128)(2,1)S(1)}, bf16[32,7168]{1,0:T(8,128)(2,1)S(1)}, u32[]{:S(2)}, u32[]{:S(2)}) collective-permute-start(bf16[32,7168]{1,0:T(8,128)(2,1)S(1)} %add_convert_fusion), channel_id=1, source_target_pairs={{0,1},{1,3},{3,2},{2,0},{4,5},{5,7},{7,6},{6,4},{8,9},{9,11},{11,1... | collective-permute-start | bytes 1376264 | tf_op jit(solution)/shard_map/ppermute | solution.py:337
  32.9 7.9 %collective-permute-start.4 = (f32[64,1024]{1,0:T(8,128)S(1)}, f32[64,1024]{1,0:T(8,128)S(1)}, u32[]{:S(2)}, u32[]{:S(2)}) collective-permute-start(f32[64,1024]{1,0:T(8,128)S(1)} %get-tuple-element.40), channel_id=1, source_target_pairs={{0,4},{4,0},{1,5},{5,1},{2,6},{6,2},{3,7},{7,3},{8,12},{12,8},{9,1... | collective-permute-start | bytes 786440 | tf_op jit(solution)/shard_map/ppermute | solution.py:342
  40.0 1.8 %collective-permute-start.7 = (bf16[128,1792]{1,0:T(8,128)(2,1)S(1)}, bf16[128,1792]{1,0:T(8,128)(2,1)S(1)}, u32[]{:S(2)}, u32[]{:S(2)}) collective-permute-start(bf16[128,1792]{1,0:T(8,128)(2,1)S(1)} %get-tuple-element.45), channel_id=1, source_target_pairs={{0,8},{8,0},{16,24},{24,16},{1,9},{9,1},{17,25},{25,17},{2,10},{10... | collective-permute-start | bytes 1376264 | tf_op jit(solution)/shard_map/ppermute | solution.py:341
  40.1 2.4 %collective-permute-start.8 = (bf16[128,1792]{1,0:T(8,128)(2,1)S(1)}, bf16[128,1792]{1,0:T(8,128)(2,1)S(1)}, u32[]{:S(2)}, u32[]{:S(2)}) collective-permute-start(bf16[128,1792]{1,0:T(8,128)(2,1)S(1)} %slice.4), channel_id=1, source_target_pairs={{0,8},{8,0},{16,24},{24,16},{1,9},{9,1},{17,25},{25,17},{2,10},{10... | collective-permute-start | bytes 1376264 | tf_op jit(solution)/shard_map/ppermute | solution.py:343

commit v4 on v3

--- a/solution.py
+++ b/solution.py
@@ -14,12 +14,14 @@
 ROUND_THREE = ((0, 1), (1, 3), (3, 2), (2, 0))
 SWAP = ((0, 1), (1, 0))
 FAR = ((0, 2), (1, 3), (2, 0), (3, 1))
+ACROSS = ((0, 3), (1, 2), (2, 1), (3, 0))
 NEAR = ((0, 1), (1, 0), (2, 3), (3, 2))
 
 VMEM = pl.BlockSpec(memory_space=pltpu.VMEM)
 HBM = pl.BlockSpec(memory_space=pltpu.HBM)
 MIB = 2**20
 CHUNK = 256
+WEIGHT_GRAD_PIECES = 7
 NO_COST = pl.CostEstimate(flops=0, bytes_accessed=0, transcendentals=0)
 
 
@@ -33,13 +35,6 @@
 
 def in_vmem(array):
     return pltpu.with_memory_space_constraint(array, pltpu.VMEM)
-
-
-def settled(array):
-    top = lax.axis_index("row") == 0
-    turned = lax.optimization_barrier(-array)
-    turned = lax.optimization_barrier(jnp.where(top, -turned, turned))
-    return lax.optimization_barrier(jnp.where(top, turned, -turned))
 
 
 def silu_product(gate, up):
@@ -52,10 +47,10 @@
 
 
 def first_kernel(
-    gate_hbm, up_hbm, weight_hbm, far_ref, weight_ref, gate_ref, up_ref, weight_sem, gate_sems, up_sems
+    gate_hbm, up_hbm, weight_hbm, across_ref, beside_ref, weight_ref, gate_ref, up_ref, weight_sem, gate_sems, up_sems
 ):
     me = lax.axis_index("dp")
-    tokens, shard = gate_ref.shape[1:]
+    shard = gate_ref.shape[2]
     half = weight_ref.shape[0]
 
     def gate_copy(i):
@@ -73,10 +68,10 @@
         gate_copy(i).start()
         up_copy(i).start()
     load.start()
-    for i in range(2):
+    for i, hidden_ref in enumerate((across_ref, beside_ref)):
         gate_copy(i).wait()
         up_copy(i).wait()
-        far_ref[i * tokens : (i + 1) * tokens] = silu_product(gate_ref[i], up_ref[i])
+        hidden_ref[...] = silu_product(gate_ref[i], up_ref[i])
     load.wait()
 
 
@@ -84,11 +79,12 @@
     tokens, units = gate_pre.shape
     features = down_weight.shape[1]
     shard = units // 4
+    hidden = jax.ShapeDtypeStruct((tokens, shard), jnp.bfloat16)
     return pl.pallas_call(
         first_kernel,
         in_specs=[HBM] * 3,
-        out_specs=[VMEM] * 2,
-        out_shape=[jax.ShapeDtypeStruct((2 * tokens, shard), jnp.bfloat16), pltpu.VMEM((units // 2, features), jnp.bfloat16)],
+        out_specs=[VMEM] * 3,
+        out_shape=[hidden, hidden, pltpu.VMEM((units // 2, features), jnp.bfloat16)],
         scratch_shapes=[
             pltpu.VMEM((2, tokens, shard), jnp.bfloat16),
             pltpu.VMEM((2, tokens, shard), jnp.bfloat16),
@@ -169,7 +165,7 @@
 
 
 def mixed_kernel(
-    gate_hbm, up_hbm, weight_hbm, far_ref,
+    gate_hbm, up_hbm, weight_hbm, across_ref, beside_ref,
     near_ref, mine_ref, keep_ref, send_ref, gate_factor_ref, up_factor_ref,
     weight_ref, gate_ref, up_ref, gate_rows_ref, up_rows_ref, total_ref,
     weight_sems, gate_sems, up_sems, row_sems,
@@ -178,7 +174,7 @@
     tokens, shard = mine_ref.shape
     tok_rows = gate_rows_ref.shape[0]
     places = (me ^ 3, me ^ 2, me ^ 1, me)
-    refs = (far_ref.at[:tokens], far_ref.at[tokens:], near_ref, mine_ref)
+    refs = (across_ref, beside_ref, near_ref, mine_ref)
 
     def gate_copy(i):
         return pltpu.make_async_copy(
@@ -236,7 +232,7 @@
     send_ref[...] = total_ref[pl.ds(pl.multiple_of((1 - row) * half, half), half)]
 
 
-def mixed_and_factors(gate_pre, up_pre, down_weight, far):
+def mixed_and_factors(gate_pre, up_pre, down_weight, across, beside):
     tokens, units = gate_pre.shape
     shard = units // 4
     features = down_weight.shape[1]
@@ -246,7 +242,7 @@
     factor = jax.ShapeDtypeStruct((tok_rows, units), jnp.float32)
     return pl.pallas_call(
         mixed_kernel,
-        in_specs=[HBM] * 3 + [VMEM],
+        in_specs=[HBM] * 3 + [VMEM] * 2,
         out_specs=[VMEM] * 6,
         out_shape=[hidden, hidden, partial, partial, factor, factor],
         scratch_shapes=[
@@ -264,40 +260,47 @@
         compiler_params=pltpu.CompilerParams(vmem_limit_bytes=32 * MIB),
         cost_estimate=NO_COST,
         name="mixed",
-    )(in_hbm(gate_pre), in_hbm(up_pre), in_hbm(down_weight), far)
-
-
-def weight_grad_kernel(scale, mine, far, near, both, cot_own, cot_far, cot_near, out):
-    tokens = mine.shape[0]
-    hidden = jnp.concatenate([mine[...], far[tokens:], near[...], both[...]], axis=0)
+    )(in_hbm(gate_pre), in_hbm(up_pre), in_hbm(down_weight), across, beside)
+
+
+def weight_grad_kernel(scale, hidden_ref, cot_own, cot_far, cot_near, out_hbm, buffer, sems):
     cotangent = jnp.concatenate([cot_own[...], cot_far[...], cot_near[...]], axis=0)
-    out[...] = lax.dot_general(
-        hidden, cotangent, (((0,), (0,)), ((), ())), preferred_element_type=jnp.float32
-    ) * jnp.float32(scale)
-
-
-def weight_grad_shard(mine, far, near, both, cot_own, cot_far, cot_near):
-    tokens, shard = mine.shape
+    shard = hidden_ref.shape[1]
+    size = shard // sems.shape[0]
+
+    def copy_out(i):
+        rows = pl.ds(i * size, size)
+        return pltpu.make_async_copy(buffer.at[rows], out_hbm.at[rows], sems.at[i])
+
+    for i in range(sems.shape[0]):
+        buffer[i * size : (i + 1) * size] = lax.dot_general(
+            hidden_ref[:, i * size : (i + 1) * size],
+            cotangent,
+            (((0,), (0,)), ((), ())),
+            preferred_element_type=jnp.float32,
+        ) * jnp.float32(scale)
+        copy_out(i).start()
+    for i in range(sems.shape[0]):
+        copy_out(i).wait()
+
+
+def weight_grad_shard(hidden, cot_own, cot_far, cot_near):
+    shard = hidden.shape[1]
     features = cot_own.shape[1]
-    size = 896 if shard % 896 == 0 else shard
-
-    def columns(array):
-        return pl.BlockSpec((array.shape[0], size), lambda i: (0, i))
-
-    def whole(array):
-        return pl.BlockSpec(array.shape, lambda i: (0, 0))
-
+    pieces = WEIGHT_GRAD_PIECES if shard % (128 * WEIGHT_GRAD_PIECES) == 0 else 1
     return pl.pallas_call(
         functools.partial(weight_grad_kernel, 0.25),
-        grid=(shard // size,),
-        in_specs=[columns(x) for x in (mine, far, near, both)]
-        + [whole(x) for x in (cot_own, cot_far, cot_near)],
-        out_specs=pl.BlockSpec((size, features), lambda i: (i, 0)),
+        in_specs=[VMEM] * 4,
+        out_specs=HBM,
         out_shape=jax.ShapeDtypeStruct((shard, features), jnp.float32),
+        scratch_shapes=[
+            pltpu.VMEM((shard, features), jnp.float32),
+            pltpu.SemaphoreType.DMA((pieces,)),
+        ],
         compiler_params=pltpu.CompilerParams(vmem_limit_bytes=24 * MIB),
         cost_estimate=NO_COST,
         name="weight_grad",
-    )(mine, far, near, both, cot_own, cot_far, cot_near)
+    )(hidden, cot_own, cot_far, cot_near)
 
 
 def gradient_factors(gate_pre, up_pre):
@@ -313,9 +316,8 @@
 
 
 def body_line(gate_pre, up_pre, down_weight, cotangent):
-    tokens = gate_pre.shape[0]
     cot_other = lax.ppermute(cotangent, "row", SWAP)
-    hidden_far, low = hidden_far_and_weight(gate_pre, up_pre, down_weight)
+    hidden_across, hidden_beside, low = hidden_far_and_weight(gate_pre, up_pre, down_weight)
 
     cot_full, ends, middle, second, third, mine = hidden_grad_parts(
         cotangent, cot_other, low, down_weight
@@ -323,31 +325,34 @@
     from_end = lax.ppermute(ends, "col", ENDS)
     from_middle = lax.ppermute(middle, "col", MIDDLE)
     from_second = lax.ppermute(second, "col", ROUND_TWO)
-    far = lax.ppermute(after(hidden_far, mine), "dp", FAR)
+    across = lax.ppermute(after(hidden_across, mine), "dp", ACROSS)
+    beside = lax.ppermute(after(hidden_beside, mine), "dp", FAR)
 
     cot_far = lax.ppermute(after(cot_full, mine), "dp", FAR)
-    hidden_near, hidden_mine, keep, send, gate_factor, up_factor = mixed_and_factors(
-        gate_pre, up_pre, down_weight, after(hidden_far, cot_far)
-    )
     place = lax.axis_index("col")
     transit = jnp.where((place == 1) | (place == 2), from_end, jnp.zeros_like(from_end))
     forward = (
-        after(third, from_middle, keep).astype(jnp.float32) + transit.astype(jnp.float32)
+        after(third, from_middle).astype(jnp.float32) + transit.astype(jnp.float32)
     ).astype(jnp.bfloat16)
     from_third = lax.ppermute(forward, "col", ROUND_THREE)
-
-    cot_far = settled(cot_far)
+    hidden_near, hidden_mine, keep, send, gate_factor, up_factor = mixed_and_factors(
+        gate_pre, up_pre, down_weight, after(hidden_across, cot_far, forward), hidden_beside
+    )
+
     cot_near = lax.ppermute(jnp.concatenate([cot_full, cot_far], axis=0), "dp", NEAR)
-    near = lax.ppermute(after(hidden_near, forward), "dp", NEAR)
-    mixed = (after(keep, forward) + lax.ppermute(after(send, forward), "row", SWAP)).astype(jnp.bfloat16)
-    both = lax.ppermute(far[:tokens], "dp", NEAR)
-    weight_grad = weight_grad_shard(hidden_mine, far, near, both, cot_full, cot_far, cot_near)
-
+    near = lax.ppermute(after(hidden_near, forward, beside), "dp", NEAR)
+    other_half = lax.ppermute(after(send, forward), "row", SWAP)
+    hidden_all = lax.optimization_barrier(
+        jnp.concatenate([hidden_mine, beside, near, across], axis=0)
+    )
+    weight_grad = weight_grad_shard(hidden_all, cot_full, cot_far, cot_near)
+
+    mixed = (after(keep, weight_grad) + other_half).astype(jnp.bfloat16)
     so_far = (
         mine.astype(jnp.float32) + from_middle.astype(jnp.float32) + from_second.astype(jnp.float32)
     )
     so_far = lax.optimization_barrier((so_far, weight_grad))[0]
-    hidden_share = so_far + after(from_third, weight_grad).astype(jnp.float32)
+    hidden_share = so_far + after(from_third, weight_grad, mixed).astype(jnp.float32)
     gate_grad = (hidden_share * gate_factor).astype(jnp.bfloat16)
     up_grad = (hidden_share * up_factor).astype(jnp.bfloat16)
     return (mixed, gate_grad, up_grad, weight_grad)

time: 50.7 us -> 50.2 us (level)
  waiting for transfers between devices: 11.2 us -> 9.84 us
  starting transfers between devices: 14.6 us -> 15.5 us
    ppermute x1, waiting for transfers between devices: 0.53 us -> 7.21 us  [body_line(): cot_far = lax.ppermute(after(cot_full, mine), 'dp', FAR)]
    ppermute x4, waiting for transfers between devices: 6.67 us -> 0.65 us  [the longest x1 0.5 us: body_line(): across = lax.ppermute(after(hidden_across, mine), 'dp', ACROSS)]
    ppermute x1, waiting for transfers between devices: 2.56 us -> 0.27 us  [body_line(): from_third = lax.ppermute(forward, 'col', ROUND_THREE)]
    add x1, other arithmetic: 0.15 us -> 1.17 us  [body_line(): mine.astype(jnp.float32) + from_middle.astype(jnp.float32)]
    ppermute x1, starting transfers between devices: 2.07 us -> 3.09 us  [body_line(): from_third = lax.ppermute(forward, 'col', ROUND_THREE)]
    neg x1 -> x0, other arithmetic: 1 us -> none  [settled(): turned = lax.optimization_barrier(-array)]
    pallas_call x3, Pallas kernels: 15.9 us -> 15 us  [the longest x1 7.71 us: mixed_and_factors(): pl.pallas_call(mixed_kernel, in_specs=[HBM] * 3 + [VMEM] * 2, out_specs=[...]
    ppermute x1, starting transfers between devices: 0.68 us -> 1.43 us  [body_line(): from_middle = lax.ppermute(middle, 'col', MIDDLE)]
  transfers between devices with their start and end apart: 11 -> 11, of which waited for: 6 -> 5; matrix products, arithmetic and copies ran while one was open for 4% -> 4% of each run, Pallas kernels for 31% -> 30%
where the time goes in v4:
time: 50.2 us; the launch traced here: 49.9 us
  Pallas kernels  20.5 us (41%)
  starting transfers between devices  15.5 us (31%)
  waiting for transfers between devices  9.84 us (20%)
  other arithmetic  3.22 us (6%)
  between operations  0.75 us (1%)
    pallas_call x1, Pallas kernels, mixed_and_factors(): pl.pallas_call(mixed_kernel, in_specs=[HBM] * 3 + [VMEM] * 2, out_specs=[...  7.71 us
    ppermute x1, waiting for transfers between devices, body_line(): cot_far = lax.ppermute(after(cot_full, mine), 'dp', FAR)  7.21 us
    pallas_call x1, Pallas kernels, hidden_grad_parts(): pl.pallas_call(hidden_grad_kernel, in_specs=[VMEM, VMEM, VMEM, HBM], out_...  5.55 us
    ppermute x1, starting transfers between devices, body_line(): from_end = lax.ppermute(ends, 'col', ENDS)  3.88 us
    pallas_call x1, Pallas kernels, hidden_far_and_weight(): pl.pallas_call(first_kernel, in_specs=[HBM] * 3, out_specs=[VMEM] * 3, ou...  3.74 us
    pallas_call x1, Pallas kernels, weight_grad_shard(): pl.pallas_call(functools.partial(weight_grad_kernel, 0.25), in_specs=[VME...  3.5 us
    ppermute x1, starting transfers between devices, body_line(): from_third = lax.ppermute(forward, 'col', ROUND_THREE)  3.09 us
    ppermute x1, starting transfers between devices, body_line(): cot_other = lax.ppermute(cotangent, 'row', SWAP)  3 us
  transfers between devices with their start and end apart: 11, of which 5 were waited for; matrix products, arithmetic and copies ran while one was open for 4% of the time, Pallas kernels for 30%

profile of v4, /device:TPU:0, one launch (start us, length us, event | category | flops | bytes accessed | tf_op | source)
XLA Modules:
  0.0 49.9 jit_solution(5149169501675733381)
XLA Ops:
  0.6 0.0 copy-start
  0.6 3.0 %collective-permute-start = (bf16[64,1024]{1,0:T(8,128)(2,1)}, bf16[64,1024]{1,0:T(8,128)(2,1)S(1)}, u32[]{:S(2)}, u32[]{:S(2)}) collective-permute-start(bf16[64,1024]{1,0:T(8,128)(2,1)} %own_ref.1), channel_id=1, source_target_pairs={{0,4},{4,0},{1,5},{5,1},{2,6},{6,2},{3,7},{7,3},{8,12},{12,8},{9,1... | collective-permute-start | bytes 393224 | tf_op jit(solution)/shard_map/ppermute | solution.py:319
  3.6 3.7 %hidden_far.1 = (bf16[128,1792]{1,0:T(8,128)(2,1)S(1)}, bf16[128,1792]{1,0:T(8,128)(2,1)S(1)}, bf16[3584,1024]{1,0:T(8,128)(2,1)S(1)}) custom-call(bf16[128,7168]{1,0:T(8,128)(2,1)} %gate_hbm.3, bf16[128,7168]{1,0:T(8,128)(2,1)} %up_hbm.3, bf16[7168,1024]{1,0:T(8,128)(2,1)} %weight_hbm.5), custom_call_target="tpu_custom_call" | custom-call | tf_op jit(solution)/shard_map/hidden_far/pallas_call | solution.py:83
  7.4 0.0 collective-permute-done.other_ref
  7.4 0.0 copy-done
  7.4 5.5 %hidden_grad.1 = (bf16[128,1024]{1,0:T(8,128)(2,1)S(1)}, bf16[32,7168]{1,0:T(8,128)(2,1)S(1)}, bf16[32,7168]{1,0:T(8,128)(2,1)}, bf16[32,7168]{1,0:T(8,128)(2,1)...) custom-call(bf16[64,1024]{1,0:T(8,128)(2,1)S(1)} %copy-done, ...), custom_call_target="tpu_custom_call" | custom-call | tf_op jit(solution)/shard_map/hidden_grad/pallas_call | solution.py:151
  13.0 1.4 %collective-permute-start.2 = (bf16[32,7168]{1,0:T(8,128)(2,1)}, bf16[32,7168]{1,0:T(8,128)(2,1)}, u32[]{:S(2)}, u32[]{:S(2)}) collective-permute-start(bf16[32,7168]{1,0:T(8,128)(2,1)} %get-tuple-element.35), channel_id=1, source_target_pairs={{1,2},{2,1},{5,6},{6,5},{9,10},{10,9},{13,14},{14,13},{17,18},{18,... | collective-permute-start | bytes 1376264 | tf_op jit(solution)/shard_map/ppermute | solution.py:326
  14.4 3.9 %collective-permute-start.3 = (bf16[32,7168]{1,0:T(8,128)(2,1)S(1)}, bf16[32,7168]{1,0:T(8,128)(2,1)}, u32[]{:S(2)}, u32[]{:S(2)}) collective-permute-start(bf16[32,7168]{1,0:T(8,128)(2,1)S(1)} %get-tuple-element.37), channel_id=1, source_target_pairs={{0,1},{1,0},{2,3},{3,2},{4,5},{5,4},{6,7},{7,6},{8,9},{9,8},{10,11... | collective-permute-start | bytes 1376264 | tf_op jit(solution)/shard_map/ppermute | solution.py:325
  18.3 1.5 %collective-permute-start.1 = (bf16[128,1024]{1,0:T(8,128)(2,1)S(1)}, bf16[128,1024]{1,0:T(8,128)(2,1)S(1)}, u32[]{:S(2)}, u32[]{:S(2)}) collective-permute-start(bf16[128,1024]{1,0:T(8,128)(2,1)S(1)} %get-tuple-element.33.cot_own), channel_id=1, source_target_pairs={{0,16},{8,24},{16,0},{24,8},{1,17},{9,25},{17,1},{25,9},{2,18},{10... | collective-permute-start | bytes 786440 | tf_op jit(solution)/shard_map/ppermute | solution.py:331
  19.8 0.5 %collective-permute-start.4 = (bf16[128,1792]{1,0:T(8,128)(2,1)S(1)}, bf16[128,1792]{1,0:T(8,128)(2,1)S(1)}, u32[]{:S(2)}, u32[]{:S(2)}) collective-permute-start(bf16[128,1792]{1,0:T(8,128)(2,1)S(1)} %get-tuple-element.42.beside_ref), channel_id=1, source_target_pairs={{0,16},{8,24},{16,0},{24,8},{1,17},{9,25},{17,1},{25,9},{2,18},{10... | collective-permute-start | bytes 1376264 | tf_op jit(solution)/shard_map/ppermute | solution.py:329
  20.3 0.0 collective-permute-start.6
  20.3 7.2 %collective-permute-done.1.cot_far = bf16[128,1024]{1,0:T(8,128)(2,1)S(1)} collective-permute-done((bf16[128,1024]{1,0:T(8,128)(2,1)S(1)}, bf16[128,1024]{1,0:T(8,128)(2,1)S(1)}, u32[]{:S(2)}, u32[]{:S(2)}) %collective-permute-start.1) | collective-permute-done | bytes 262176 | tf_op jit(solution)/shard_map/ppermute | solution.py:331
  27.5 0.5 collective-permute-start.9
  28.0 0.0 collective-permute-done.2
  28.0 0.1 collective-permute-start.7
  28.1 1.7 %collective-permute-done.3 = bf16[32,7168]{1,0:T(8,128)(2,1)} collective-permute-done((bf16[32,7168]{1,0:T(8,128)(2,1)S(1)}, bf16[32,7168]{1,0:T(8,128)(2,1)}, u32[]{:S(2)}, u32[]{:S(2)}) %collective-permute-start.3) | collective-permute-done | bytes 458784 | tf_op jit(solution)/shard_map/ppermute | solution.py:325
  29.8 0.1 add_convert_fusion
  30.0 3.1 %collective-permute-start.10 = (bf16[32,7168]{1,0:T(8,128)(2,1)S(1)}, bf16[32,7168]{1,0:T(8,128)(2,1)S(1)}, u32[]{:S(2)}, u32[]{:S(2)}) collective-permute-start(bf16[32,7168]{1,0:T(8,128)(2,1)S(1)} %add_convert_fusion), channel_id=1, source_target_pairs={{0,1},{1,3},{3,2},{2,0},{4,5},{5,7},{7,6},{6,4},{8,9},{9,11},{11,1... | collective-permute-start | bytes 1376264 | tf_op jit(solution)/shard_map/ppermute | solution.py:337
  33.1 7.7 %mixed.1 = (bf16[128,1792]{1,0:T(8,128)(2,1)S(1)}, bf16[128,1792]{1,0:T(8,128)(2,1)S(1)}, f32[64,1024]{1,0:T(8,128)S(1)}, f32[64,1024]{1,0:T(8,128)S(1)}, f32[32...) custom-call(bf16[128,7168]{1,0:T(8,128)(2,1)} %gate_hbm.3, bf16[128,7168]{1,0:T(8,128)(2,1)} %up_hbm.3, ...), custom_call_target="tpu_custom_call" | custom-call | tf_op jit(solution)/shard_map/mixed/pallas_call | solution.py:243
  40.8 0.0 collective-permute-done.4
  40.8 1.6 %collective-permute-start.8 = (f32[64,1024]{1,0:T(8,128)S(1)}, f32[64,1024]{1,0:T(8,128)S(1)}, u32[]{:S(2)}, u32[]{:S(2)}) collective-permute-start(f32[64,1024]{1,0:T(8,128)S(1)} %get-tuple-element.48), channel_id=1, source_target_pairs={{0,4},{4,0},{1,5},{5,1},{2,6},{6,2},{3,7},{7,3},{8,12},{12,8},{9,1... | collective-permute-start | bytes 786440 | tf_op jit(solution)/shard_map/ppermute | solution.py:344
  42.4 0.0 collective-permute-done.9
  42.4 0.0 collective-permute-start.5
  42.4 1.2 %convert_add_fusion.1 = f32[32,7168]{1,0:T(8,128)S(1)} fusion(bf16[32,7168]{1,0:T(8,128)(2,1)S(1)} %collective-permute-done.9, bf16[32,7168]{1,0:T(8,128)(2,1)} %collective-permute-done.2, bf16[32,7168]{1,0:T(8,128)(2,1)S(1)} %get-tuple-element.32), kind=kLoop, calls=%fused_computation.4 | loop fusion | flops 1146880 | bytes 2293760 | tf_op jit(solution)/shard_map/add | solution.py:352
  43.5 0.5 collective-permute-done.6
  44.0 0.1 collective-permute-done.5
  44.2 0.1 pad_maximum_fusion.hidden_ref
  44.3 0.0 collective-permute-done.7.cot_near
  44.3 3.5 %weight_grad.1 = f32[1792,1024]{1,0:T(8,128)} custom-call(bf16[512,1792]{1,0:T(8,128)(2,1)S(1)} %pad_maximum_fusion.hidden_ref, bf16[128,1024]{1,0:T(8,128)(2,1)S(1)} %get-tuple-element.33.cot_own, bf16[128,1024]{1,0:T(8,128)(2,1)S(1)} %collective-permute-done.1.cot_far, bf16[256,1024]{1,0:T(8,128)(2,1)S(1)} %collective-permute-done.7.cot_near), custom_call_target="tpu_custom_call" | custom-call | tf_op jit(solution)/shard_map/weight_grad/pallas_call | solution.py:291
  47.8 0.0 collective-permute-done.8
  47.8 0.7 %add_convert_fusion.1 = bf16[64,1024]{1,0:T(8,128)(2,1)} fusion(f32[64,1024]{1,0:T(8,128)S(1)} %get-tuple-element.46, f32[64,1024]{1,0:T(8,128)S(1)} %collective-permute-done.8), kind=kLoop, calls=%fused_computation.7 | loop fusion | flops 131072 | bytes 655360 | tf_op jit(solution)/shard_map/convert_element_type | solution.py:350
  48.5 0.3 collective-permute-done.10
  48.8 1.1 %multiply_convert_fusion = (bf16[32,7168]{1,0:T(8,128)(2,1)}, bf16[32,7168]{1,0:T(8,128)(2,1)}) fusion(f32[32,7168]{1,0:T(8,128)S(1)} %get-tuple-element.53, f32[32,7168]{1,0:T(8,128)S(1)} %convert_add_fusion.1, bf16[32,7168]{1,0:T(8,128)(2,1)S(1)} %collective-permute-done.10, f32[32,7168]{1,0:T(8,128)S(1)} %get-tuple-element.52), kind=kLoop, calls=%fused_computation.1 | loop fusion | flops 1376256 | bytes 4128768 | tf_op jit(solution)/shard_map/convert_element_type | solution.py:357
  (1 shorter events, 0.0 us)
Async XLA Ops:
  0.6 6.8 %copy-start = (bf16[64,1024]{1,0:T(8,128)(2,1)S(1)}, bf16[64,1024]{1,0:T(8,128)(2,1)}, u32[]{:S(2)}) copy-start(bf16[64,1024]{1,0:T(8,128)(2,1)} %own_ref.1) | copy-start | bytes 393220
  0.6 6.8 %collective-permute-start = (bf16[64,1024]{1,0:T(8,128)(2,1)}, bf16[64,1024]{1,0:T(8,128)(2,1)S(1)}, u32[]{:S(2)}, u32[]{:S(2)}) collective-permute-start(bf16[64,1024]{1,0:T(8,128)(2,1)} %own_ref.1), channel_id=1, source_target_pairs={{0,4},{4,0},{1,5},{5,1},{2,6},{6,2},{3,7},{7,3},{8,12},{12,8},{9,1... | collective-permute-start | bytes 393224 | tf_op jit(solution)/shard_map/ppermute | solution.py:319
  13.0 15.1 %collective-permute-start.2 = (bf16[32,7168]{1,0:T(8,128)(2,1)}, bf16[32,7168]{1,0:T(8,128)(2,1)}, u32[]{:S(2)}, u32[]{:S(2)}) collective-permute-start(bf16[32,7168]{1,0:T(8,128)(2,1)} %get-tuple-element.35), channel_id=1, source_target_pairs={{1,2},{2,1},{5,6},{6,5},{9,10},{10,9},{13,14},{14,13},{17,18},{18,... | collective-permute-start | bytes 1376264 | tf_op jit(solution)/shard_map/ppermute | solution.py:326
  14.4 15.4 %collective-permute-start.3 = (bf16[32,7168]{1,0:T(8,128)(2,1)S(1)}, bf16[32,7168]{1,0:T(8,128)(2,1)}, u32[]{:S(2)}, u32[]{:S(2)}) collective-permute-start(bf16[32,7168]{1,0:T(8,128)(2,1)S(1)} %get-tuple-element.37), channel_id=1, source_target_pairs={{0,1},{1,0},{2,3},{3,2},{4,5},{5,4},{6,7},{7,6},{8,9},{9,8},{10,11... | collective-permute-start | bytes 1376264 | tf_op jit(solution)/shard_map/ppermute | solution.py:325
  18.3 9.2 %collective-permute-start.1 = (bf16[128,1024]{1,0:T(8,128)(2,1)S(1)}, bf16[128,1024]{1,0:T(8,128)(2,1)S(1)}, u32[]{:S(2)}, u32[]{:S(2)}) collective-permute-start(bf16[128,1024]{1,0:T(8,128)(2,1)S(1)} %get-tuple-element.33.cot_own), channel_id=1, source_target_pairs={{0,16},{8,24},{16,0},{24,8},{1,17},{9,25},{17,1},{25,9},{2,18},{10... | collective-permute-start | bytes 786440 | tf_op jit(solution)/shard_map/ppermute | solution.py:331
  19.8 21.0 %collective-permute-start.4 = (bf16[128,1792]{1,0:T(8,128)(2,1)S(1)}, bf16[128,1792]{1,0:T(8,128)(2,1)S(1)}, u32[]{:S(2)}, u32[]{:S(2)}) collective-permute-start(bf16[128,1792]{1,0:T(8,128)(2,1)S(1)} %get-tuple-element.42.beside_ref), channel_id=1, source_target_pairs={{0,16},{8,24},{16,0},{24,8},{1,17},{9,25},{17,1},{25,9},{2,18},{10... | collective-permute-start | bytes 1376264 | tf_op jit(solution)/shard_map/ppermute | solution.py:329
  20.3 23.7 %collective-permute-start.6 = (bf16[128,1792]{1,0:T(8,128)(2,1)S(1)}, bf16[128,1792]{1,0:T(8,128)(2,1)S(1)}, u32[]{:S(2)}, u32[]{:S(2)}) collective-permute-start(bf16[128,1792]{1,0:T(8,128)(2,1)S(1)} %get-tuple-element.45.across_ref), channel_id=1, source_target_pairs={{0,24},{8,16},{16,8},{24,0},{1,25},{9,17},{17,9},{25,1},{2,26},{10... | collective-permute-start | bytes 1376264 | tf_op jit(solution)/shard_map/ppermute | solution.py:328
  27.5 14.8 %collective-permute-start.9 = (bf16[32,7168]{1,0:T(8,128)(2,1)S(1)}, bf16[32,7168]{1,0:T(8,128)(2,1)S(1)}, u32[]{:S(2)}, u32[]{:S(2)}) collective-permute-start(bf16[32,7168]{1,0:T(8,128)(2,1)S(1)} %get-tuple-element.49), channel_id=1, source_target_pairs={{0,2},{2,3},{3,1},{1,0},{4,6},{6,7},{7,5},{5,4},{8,10},{10,11},{11... | collective-permute-start | bytes 1376264 | tf_op jit(solution)/shard_map/ppermute | solution.py:327
  28.0 16.3 %collective-permute-start.7 = (bf16[256,1024]{1,0:T(8,128)(2,1)S(1)}, bf16[256,1024]{1,0:T(8,128)(2,1)S(1)}, u32[]{:S(2)}, u32[]{:S(2)}) collective-permute-start(bf16[256,1024]{1,0:T(8,128)(2,1)S(1)} %pad_maximum_fusion.1), channel_id=1, source_target_pairs={{0,8},{8,0},{16,24},{24,16},{1,9},{9,1},{17,25},{25,17},{2,10},{10... | collective-permute-start | bytes 1572872 | tf_op jit(solution)/shard_map/ppermute | solution.py:342
  30.0 18.8 %collective-permute-start.10 = (bf16[32,7168]{1,0:T(8,128)(2,1)S(1)}, bf16[32,7168]{1,0:T(8,128)(2,1)S(1)}, u32[]{:S(2)}, u32[]{:S(2)}) collective-permute-start(bf16[32,7168]{1,0:T(8,128)(2,1)S(1)} %add_convert_fusion), channel_id=1, source_target_pairs={{0,1},{1,3},{3,2},{2,0},{4,5},{5,7},{7,6},{6,4},{8,9},{9,11},{11,1... | collective-permute-start | bytes 1376264 | tf_op jit(solution)/shard_map/ppermute | solution.py:337
  40.8 7.0 %collective-permute-start.8 = (f32[64,1024]{1,0:T(8,128)S(1)}, f32[64,1024]{1,0:T(8,128)S(1)}, u32[]{:S(2)}, u32[]{:S(2)}) collective-permute-start(f32[64,1024]{1,0:T(8,128)S(1)} %get-tuple-element.48), channel_id=1, source_target_pairs={{0,4},{4,0},{1,5},{5,1},{2,6},{6,2},{3,7},{7,3},{8,12},{12,8},{9,1... | collective-permute-start | bytes 786440 | tf_op jit(solution)/shard_map/ppermute | solution.py:344
  42.4 1.8 %collective-permute-start.5 = (bf16[128,1792]{1,0:T(8,128)(2,1)S(1)}, bf16[128,1792]{1,0:T(8,128)(2,1)S(1)}, u32[]{:S(2)}, u32[]{:S(2)}) collective-permute-start(bf16[128,1792]{1,0:T(8,128)(2,1)S(1)} %get-tuple-element.44), channel_id=1, source_target_pairs={{0,8},{8,0},{16,24},{24,16},{1,9},{9,1},{17,25},{25,17},{2,10},{10... | collective-permute-start | bytes 1376264 | tf_op jit(solution)/shard_map/ppermute | solution.py:343

commit v5 on v4

--- a/solution.py
+++ b/solution.py
@@ -20,7 +20,7 @@
 VMEM = pl.BlockSpec(memory_space=pltpu.VMEM)
 HBM = pl.BlockSpec(memory_space=pltpu.HBM)
 MIB = 2**20
-CHUNK = 256
+CHUNK = 896
 WEIGHT_GRAD_PIECES = 7
 NO_COST = pl.CostEstimate(flops=0, bytes_accessed=0, transcendentals=0)
 
@@ -99,7 +99,7 @@
 
 
 def hidden_grad_kernel(
-    own_ref, other_ref, low_ref, weight_hbm, full_ref, ends, middle, second, third, mine, ordered_ref, high_ref, sem
+    own_ref, other_ref, low_ref, weight_hbm, full_ref, ends, second, third, mine, ordered_ref, high_ref, sem
 ):
     units = low_ref.shape[0]
     quarter = units // 2
@@ -138,7 +138,6 @@
             rounded = product.astype(jnp.bfloat16).T
             columns = slice(base + start, base + start + size)
             ends[:, columns] = rounded[:tokens]
-            middle[:, columns] = rounded[:tokens]
             second[:, columns] = rounded[tokens : 2 * tokens]
             third[:, columns] = rounded[2 * tokens : 3 * tokens]
             mine[:, columns] = rounded[3 * tokens :]
@@ -151,8 +150,8 @@
     return pl.pallas_call(
         hidden_grad_kernel,
         in_specs=[VMEM, VMEM, VMEM, HBM],
-        out_specs=[VMEM] * 6,
-        out_shape=[jax.ShapeDtypeStruct((2 * half, depth), jnp.bfloat16)] + [part] * 5,
+        out_specs=[VMEM] * 5,
+        out_shape=[jax.ShapeDtypeStruct((2 * half, depth), jnp.bfloat16)] + [part] * 4,
         scratch_shapes=[
             pltpu.VMEM((2 * half, depth), jnp.bfloat16),
             pltpu.VMEM((units, depth), jnp.bfloat16),
@@ -319,11 +318,11 @@
     cot_other = lax.ppermute(cotangent, "row", SWAP)
     hidden_across, hidden_beside, low = hidden_far_and_weight(gate_pre, up_pre, down_weight)
 
-    cot_full, ends, middle, second, third, mine = hidden_grad_parts(
+    cot_full, ends, second, third, mine = hidden_grad_parts(
         cotangent, cot_other, low, down_weight
     )
     from_end = lax.ppermute(ends, "col", ENDS)
-    from_middle = lax.ppermute(middle, "col", MIDDLE)
+    from_middle = lax.ppermute(ends, "col", MIDDLE)
     from_second = lax.ppermute(second, "col", ROUND_TWO)
     across = lax.ppermute(after(hidden_across, mine), "dp", ACROSS)
     beside = lax.ppermute(after(hidden_beside, mine), "dp", FAR)
@@ -341,7 +340,7 @@
 
     cot_near = lax.ppermute(jnp.concatenate([cot_full, cot_far], axis=0), "dp", NEAR)
     near = lax.ppermute(after(hidden_near, forward, beside), "dp", NEAR)
-    other_half = lax.ppermute(after(send, forward), "row", SWAP)
+    other_half = lax.ppermute(after(send, forward).astype(jnp.bfloat16), "row", SWAP).astype(jnp.float32)
     hidden_all = lax.optimization_barrier(
         jnp.concatenate([hidden_mine, beside, near, across], axis=0)
     )

time: 50.2 us -> 49.3 us (0.982)
  Pallas kernels: 20.5 us -> 19.5 us
    pallas_call x1, Pallas kernels: 5.55 us -> 4.57 us  [hidden_grad_parts(): pl.pallas_call(hidden_grad_kernel, in_specs=[VMEM, VMEM, VMEM, HBM], out_...]
  transfers between devices with their start and end apart: 11 -> 11, of which waited for: 5 -> 5; matrix products, arithmetic and copies ran while one was open for 4% -> 4% of each run, Pallas kernels for 30% -> 31%
where the time goes in v5:
time: 49.3 us; the launch traced here: 48.9 us
  Pallas kernels  19.5 us (40%)
  starting transfers between devices  15.5 us (31%)
  waiting for transfers between devices  9.83 us (20%)
  other arithmetic  3.24 us (7%)
  between operations  0.76 us (2%)
    pallas_call x1, Pallas kernels, mixed_and_factors(): pl.pallas_call(mixed_kernel, in_specs=[HBM] * 3 + [VMEM] * 2, out_specs=[...  7.71 us
    ppermute x1, waiting for transfers between devices, body_line(): cot_far = lax.ppermute(after(cot_full, mine), 'dp', FAR)  7.22 us
    pallas_call x1, Pallas kernels, hidden_grad_parts(): pl.pallas_call(hidden_grad_kernel, in_specs=[VMEM, VMEM, VMEM, HBM], out_...  4.57 us
    ppermute x1, starting transfers between devices, body_line(): from_end = lax.ppermute(ends, 'col', ENDS)  3.86 us
    pallas_call x1, Pallas kernels, hidden_far_and_weight(): pl.pallas_call(first_kernel, in_specs=[HBM] * 3, out_specs=[VMEM] * 3, ou...  3.74 us
    pallas_call x1, Pallas kernels, weight_grad_shard(): pl.pallas_call(functools.partial(weight_grad_kernel, 0.25), in_specs=[VME...  3.5 us
    ppermute x1, starting transfers between devices, body_line(): from_third = lax.ppermute(forward, 'col', ROUND_THREE)  3.09 us
    ppermute x1, starting transfers between devices, body_line(): cot_other = lax.ppermute(cotangent, 'row', SWAP)  3 us
  transfers between devices with their start and end apart: 11, of which 5 were waited for; matrix products, arithmetic and copies ran while one was open for 4% of the time, Pallas kernels for 31%

profile of v5, /device:TPU:0, one launch (start us, length us, event | category | flops | bytes accessed | tf_op | source)
XLA Modules:
  0.0 48.9 jit_solution(10232363858010785136)
XLA Ops:
  0.6 0.0 copy-start
  0.6 3.0 %collective-permute-start = (bf16[64,1024]{1,0:T(8,128)(2,1)}, bf16[64,1024]{1,0:T(8,128)(2,1)S(1)}, u32[]{:S(2)}, u32[]{:S(2)}) collective-permute-start(bf16[64,1024]{1,0:T(8,128)(2,1)} %own_ref.1), channel_id=1, source_target_pairs={{0,4},{4,0},{1,5},{5,1},{2,6},{6,2},{3,7},{7,3},{8,12},{12,8},{9,1... | collective-permute-start | bytes 393224 | tf_op jit(solution)/shard_map/ppermute | solution.py:318
  3.6 3.7 %hidden_far.1 = (bf16[128,1792]{1,0:T(8,128)(2,1)S(1)}, bf16[128,1792]{1,0:T(8,128)(2,1)S(1)}, bf16[3584,1024]{1,0:T(8,128)(2,1)S(1)}) custom-call(bf16[128,7168]{1,0:T(8,128)(2,1)} %gate_hbm.3, bf16[128,7168]{1,0:T(8,128)(2,1)} %up_hbm.3, bf16[7168,1024]{1,0:T(8,128)(2,1)} %weight_hbm.5), custom_call_target="tpu_custom_call" | custom-call | tf_op jit(solution)/shard_map/hidden_far/pallas_call | solution.py:83
  7.4 0.0 collective-permute-done.other_ref
  7.4 0.0 copy-done
  7.4 4.6 %hidden_grad.1 = (bf16[128,1024]{1,0:T(8,128)(2,1)S(1)}, bf16[32,7168]{1,0:T(8,128)(2,1)S(1)}, bf16[32,7168]{1,0:T(8,128)(2,1)S(1)}, bf16[32,7168]{1,0:T(8,128)(2,1)S(1)}, bf16[32,7168]{1,0:T(8,128)(2,1)S(1)}) custom-call(bf16[64,1024]{1,0:T(8,128)(2,1)S(1)} %copy-done, bf16[64,1024]{1,0:T(8,128)(2,1)S(1)} %collective-permute-done.other_ref, ...), custom_call_target="tpu_custom_call" | custom-call | tf_op jit(solution)/shard_map/hidden_grad/pallas_call | solution.py:150
  12.0 1.4 %collective-permute-start.2 = (bf16[32,7168]{1,0:T(8,128)(2,1)S(1)}, bf16[32,7168]{1,0:T(8,128)(2,1)}, u32[]{:S(2)}, u32[]{:S(2)}) collective-permute-start(bf16[32,7168]{1,0:T(8,128)(2,1)S(1)} %get-tuple-element.34), channel_id=1, source_target_pairs={{1,2},{2,1},{5,6},{6,5},{9,10},{10,9},{13,14},{14,13},{17,18},{18,... | collective-permute-start | bytes 1376264 | tf_op jit(solution)/shard_map/ppermute | solution.py:325
  13.4 3.9 %collective-permute-start.3 = (bf16[32,7168]{1,0:T(8,128)(2,1)S(1)}, bf16[32,7168]{1,0:T(8,128)(2,1)}, u32[]{:S(2)}, u32[]{:S(2)}) collective-permute-start(bf16[32,7168]{1,0:T(8,128)(2,1)S(1)} %get-tuple-element.34), channel_id=1, source_target_pairs={{0,1},{1,0},{2,3},{3,2},{4,5},{5,4},{6,7},{7,6},{8,9},{9,8},{10,11... | collective-permute-start | bytes 1376264 | tf_op jit(solution)/shard_map/ppermute | solution.py:324
  17.3 1.5 %collective-permute-start.1 = (bf16[128,1024]{1,0:T(8,128)(2,1)S(1)}, bf16[128,1024]{1,0:T(8,128)(2,1)S(1)}, u32[]{:S(2)}, u32[]{:S(2)}) collective-permute-start(bf16[128,1024]{1,0:T(8,128)(2,1)S(1)} %get-tuple-element.32.cot_own), channel_id=1, source_target_pairs={{0,16},{8,24},{16,0},{24,8},{1,17},{9,25},{17,1},{25,9},{2,18},{10... | collective-permute-start | bytes 786440 | tf_op jit(solution)/shard_map/ppermute | solution.py:330
  18.8 0.5 %collective-permute-start.4 = (bf16[128,1792]{1,0:T(8,128)(2,1)S(1)}, bf16[128,1792]{1,0:T(8,128)(2,1)S(1)}, u32[]{:S(2)}, u32[]{:S(2)}) collective-permute-start(bf16[128,1792]{1,0:T(8,128)(2,1)S(1)} %get-tuple-element.40.beside_ref), channel_id=1, source_target_pairs={{0,16},{8,24},{16,0},{24,8},{1,17},{9,25},{17,1},{25,9},{2,18},{10... | collective-permute-start | bytes 1376264 | tf_op jit(solution)/shard_map/ppermute | solution.py:328
  19.3 0.0 collective-permute-start.6
  19.3 7.2 %collective-permute-done.1.cot_far = bf16[128,1024]{1,0:T(8,128)(2,1)S(1)} collective-permute-done((bf16[128,1024]{1,0:T(8,128)(2,1)S(1)}, bf16[128,1024]{1,0:T(8,128)(2,1)S(1)}, u32[]{:S(2)}, u32[]{:S(2)}) %collective-permute-start.1) | collective-permute-done | bytes 262176 | tf_op jit(solution)/shard_map/ppermute | solution.py:330
  26.5 0.5 collective-permute-start.9
  27.0 0.0 collective-permute-done.2
  27.0 0.1 collective-permute-start.7
  27.1 1.7 %collective-permute-done.3 = bf16[32,7168]{1,0:T(8,128)(2,1)} collective-permute-done((bf16[32,7168]{1,0:T(8,128)(2,1)S(1)}, bf16[32,7168]{1,0:T(8,128)(2,1)}, u32[]{:S(2)}, u32[]{:S(2)}) %collective-permute-start.3) | collective-permute-done | bytes 458784 | tf_op jit(solution)/shard_map/ppermute | solution.py:324
  28.8 0.1 add_convert_fusion
  29.0 3.1 %collective-permute-start.10 = (bf16[32,7168]{1,0:T(8,128)(2,1)S(1)}, bf16[32,7168]{1,0:T(8,128)(2,1)S(1)}, u32[]{:S(2)}, u32[]{:S(2)}) collective-permute-start(bf16[32,7168]{1,0:T(8,128)(2,1)S(1)} %add_convert_fusion), channel_id=1, source_target_pairs={{0,1},{1,3},{3,2},{2,0},{4,5},{5,7},{7,6},{6,4},{8,9},{9,11},{11,1... | collective-permute-start | bytes 1376264 | tf_op jit(solution)/shard_map/ppermute | solution.py:336
  32.1 7.7 %mixed.1 = (bf16[128,1792]{1,0:T(8,128)(2,1)S(1)}, bf16[128,1792]{1,0:T(8,128)(2,1)S(1)}, f32[64,1024]{1,0:T(8,128)S(1)}, f32[64,1024]{1,0:T(8,128)S(1)}, f32[32...) custom-call(bf16[128,7168]{1,0:T(8,128)(2,1)} %gate_hbm.3, bf16[128,7168]{1,0:T(8,128)(2,1)} %up_hbm.3, ...), custom_call_target="tpu_custom_call" | custom-call | tf_op jit(solution)/shard_map/mixed/pallas_call | solution.py:242
  39.8 0.0 collective-permute-done.4
  39.8 1.6 %collective-permute-start.8 = (bf16[64,1024]{1,0:T(8,128)(2,1)S(1)}, bf16[64,1024]{1,0:T(8,128)(2,1)S(1)}, u32[]{:S(2)}, u32[]{:S(2)}) collective-permute-start(bf16[64,1024]{1,0:T(8,128)(2,1)S(1)} %convert_element_type.39), channel_id=1, source_target_pairs={{0,4},{4,0},{1,5},{5,1},{2,6},{6,2},{3,7},{7,3},{8,12},{12,8},{9,1... | collective-permute-start | bytes 393224 | tf_op jit(solution)/shard_map/ppermute | solution.py:343
  41.4 0.0 collective-permute-done.9
  41.4 0.0 collective-permute-start.5
  41.4 1.2 %convert_add_fusion.1 = f32[32,7168]{1,0:T(8,128)S(1)} fusion(bf16[32,7168]{1,0:T(8,128)(2,1)S(1)} %collective-permute-done.9, bf16[32,7168]{1,0:T(8,128)(2,1)} %collective-permute-done.2, bf16[32,7168]{1,0:T(8,128)(2,1)S(1)} %get-tuple-element.31), kind=kLoop, calls=%fused_computation.4 | loop fusion | flops 1146880 | bytes 2293760 | tf_op jit(solution)/shard_map/add | solution.py:351
  42.6 0.5 %collective-permute-done.6 = bf16[128,1792]{1,0:T(8,128)(2,1)S(1)} collective-permute-done((bf16[128,1792]{1,0:T(8,128)(2,1)S(1)}, bf16[128,1792]{1,0:T(8,128)(2,1)S(1)}, u32[]{:S(2)}, u32[]{:S(2)}) %collective-permute-start.6) | collective-permute-done | bytes 458784 | tf_op jit(solution)/shard_map/ppermute | solution.py:327
  43.0 0.1 collective-permute-done.5
  43.2 0.1 pad_maximum_fusion.hidden_ref
  43.3 0.0 collective-permute-done.7.cot_near
  43.3 3.5 %weight_grad.1 = f32[1792,1024]{1,0:T(8,128)} custom-call(bf16[512,1792]{1,0:T(8,128)(2,1)S(1)} %pad_maximum_fusion.hidden_ref, bf16[128,1024]{1,0:T(8,128)(2,1)S(1)} %get-tuple-element.32.cot_own, bf16[128,1024]{1,0:T(8,128)(2,1)S(1)} %collective-permute-done.1.cot_far, bf16[256,1024]{1,0:T(8,128)(2,1)S(1)} %collective-permute-done.7.cot_near), custom_call_target="tpu_custom_call" | custom-call | tf_op jit(solution)/shard_map/weight_grad/pallas_call | solution.py:290
  46.8 0.0 collective-permute-done.8
  46.9 0.7 %add_convert_fusion.1 = bf16[64,1024]{1,0:T(8,128)(2,1)} fusion(f32[64,1024]{1,0:T(8,128)S(1)} %get-tuple-element.44, bf16[64,1024]{1,0:T(8,128)(2,1)S(1)} %collective-permute-done.8), kind=kLoop, calls=%fused_computation.7 | loop fusion | flops 196608 | bytes 524288 | tf_op jit(solution)/shard_map/convert_element_type | solution.py:349
  47.5 0.3 collective-permute-done.10
  47.8 1.1 %multiply_convert_fusion = (bf16[32,7168]{1,0:T(8,128)(2,1)}, bf16[32,7168]{1,0:T(8,128)(2,1)}) fusion(f32[32,7168]{1,0:T(8,128)S(1)} %get-tuple-element.51, f32[32,7168]{1,0:T(8,128)S(1)} %convert_add_fusion.1, bf16[32,7168]{1,0:T(8,128)(2,1)S(1)} %collective-permute-done.10, f32[32,7168]{1,0:T(8,128)S(1)} %get-tuple-element.50), kind=kLoop, calls=%fused_computation.1 | loop fusion | flops 1376256 | bytes 4128768 | tf_op jit(solution)/shard_map/convert_element_type | solution.py:356
  (2 shorter events, 0.1 us)
Async XLA Ops:
  0.6 6.8 %copy-start = (bf16[64,1024]{1,0:T(8,128)(2,1)S(1)}, bf16[64,1024]{1,0:T(8,128)(2,1)}, u32[]{:S(2)}) copy-start(bf16[64,1024]{1,0:T(8,128)(2,1)} %own_ref.1) | copy-start | bytes 393220
  0.6 6.8 %collective-permute-start = (bf16[64,1024]{1,0:T(8,128)(2,1)}, bf16[64,1024]{1,0:T(8,128)(2,1)S(1)}, u32[]{:S(2)}, u32[]{:S(2)}) collective-permute-start(bf16[64,1024]{1,0:T(8,128)(2,1)} %own_ref.1), channel_id=1, source_target_pairs={{0,4},{4,0},{1,5},{5,1},{2,6},{6,2},{3,7},{7,3},{8,12},{12,8},{9,1... | collective-permute-start | bytes 393224 | tf_op jit(solution)/shard_map/ppermute | solution.py:318
  12.0 15.0 %collective-permute-start.2 = (bf16[32,7168]{1,0:T(8,128)(2,1)S(1)}, bf16[32,7168]{1,0:T(8,128)(2,1)}, u32[]{:S(2)}, u32[]{:S(2)}) collective-permute-start(bf16[32,7168]{1,0:T(8,128)(2,1)S(1)} %get-tuple-element.34), channel_id=1, source_target_pairs={{1,2},{2,1},{5,6},{6,5},{9,10},{10,9},{13,14},{14,13},{17,18},{18,... | collective-permute-start | bytes 1376264 | tf_op jit(solution)/shard_map/ppermute | solution.py:325
  13.4 15.4 %collective-permute-start.3 = (bf16[32,7168]{1,0:T(8,128)(2,1)S(1)}, bf16[32,7168]{1,0:T(8,128)(2,1)}, u32[]{:S(2)}, u32[]{:S(2)}) collective-permute-start(bf16[32,7168]{1,0:T(8,128)(2,1)S(1)} %get-tuple-element.34), channel_id=1, source_target_pairs={{0,1},{1,0},{2,3},{3,2},{4,5},{5,4},{6,7},{7,6},{8,9},{9,8},{10,11... | collective-permute-start | bytes 1376264 | tf_op jit(solution)/shard_map/ppermute | solution.py:324
  17.3 9.2 %collective-permute-start.1 = (bf16[128,1024]{1,0:T(8,128)(2,1)S(1)}, bf16[128,1024]{1,0:T(8,128)(2,1)S(1)}, u32[]{:S(2)}, u32[]{:S(2)}) collective-permute-start(bf16[128,1024]{1,0:T(8,128)(2,1)S(1)} %get-tuple-element.32.cot_own), channel_id=1, source_target_pairs={{0,16},{8,24},{16,0},{24,8},{1,17},{9,25},{17,1},{25,9},{2,18},{10... | collective-permute-start | bytes 786440 | tf_op jit(solution)/shard_map/ppermute | solution.py:330
  18.8 21.0 %collective-permute-start.4 = (bf16[128,1792]{1,0:T(8,128)(2,1)S(1)}, bf16[128,1792]{1,0:T(8,128)(2,1)S(1)}, u32[]{:S(2)}, u32[]{:S(2)}) collective-permute-start(bf16[128,1792]{1,0:T(8,128)(2,1)S(1)} %get-tuple-element.40.beside_ref), channel_id=1, source_target_pairs={{0,16},{8,24},{16,0},{24,8},{1,17},{9,25},{17,1},{25,9},{2,18},{10... | collective-permute-start | bytes 1376264 | tf_op jit(solution)/shard_map/ppermute | solution.py:328
  19.3 23.7 %collective-permute-start.6 = (bf16[128,1792]{1,0:T(8,128)(2,1)S(1)}, bf16[128,1792]{1,0:T(8,128)(2,1)S(1)}, u32[]{:S(2)}, u32[]{:S(2)}) collective-permute-start(bf16[128,1792]{1,0:T(8,128)(2,1)S(1)} %get-tuple-element.43.across_ref), channel_id=1, source_target_pairs={{0,24},{8,16},{16,8},{24,0},{1,25},{9,17},{17,9},{25,1},{2,26},{10... | collective-permute-start | bytes 1376264 | tf_op jit(solution)/shard_map/ppermute | solution.py:327
  26.5 14.8 %collective-permute-start.9 = (bf16[32,7168]{1,0:T(8,128)(2,1)S(1)}, bf16[32,7168]{1,0:T(8,128)(2,1)S(1)}, u32[]{:S(2)}, u32[]{:S(2)}) collective-permute-start(bf16[32,7168]{1,0:T(8,128)(2,1)S(1)} %get-tuple-element.47), channel_id=1, source_target_pairs={{0,2},{2,3},{3,1},{1,0},{4,6},{6,7},{7,5},{5,4},{8,10},{10,11},{11... | collective-permute-start | bytes 1376264 | tf_op jit(solution)/shard_map/ppermute | solution.py:326
  27.0 16.3 %collective-permute-start.7 = (bf16[256,1024]{1,0:T(8,128)(2,1)S(1)}, bf16[256,1024]{1,0:T(8,128)(2,1)S(1)}, u32[]{:S(2)}, u32[]{:S(2)}) collective-permute-start(bf16[256,1024]{1,0:T(8,128)(2,1)S(1)} %pad_maximum_fusion.1), channel_id=1, source_target_pairs={{0,8},{8,0},{16,24},{24,16},{1,9},{9,1},{17,25},{25,17},{2,10},{10... | collective-permute-start | bytes 1572872 | tf_op jit(solution)/shard_map/ppermute | solution.py:341
  29.0 18.8 %collective-permute-start.10 = (bf16[32,7168]{1,0:T(8,128)(2,1)S(1)}, bf16[32,7168]{1,0:T(8,128)(2,1)S(1)}, u32[]{:S(2)}, u32[]{:S(2)}) collective-permute-start(bf16[32,7168]{1,0:T(8,128)(2,1)S(1)} %add_convert_fusion), channel_id=1, source_target_pairs={{0,1},{1,3},{3,2},{2,0},{4,5},{5,7},{7,6},{6,4},{8,9},{9,11},{11,1... | collective-permute-start | bytes 1376264 | tf_op jit(solution)/shard_map/ppermute | solution.py:336
  39.8 7.0 %collective-permute-start.8 = (bf16[64,1024]{1,0:T(8,128)(2,1)S(1)}, bf16[64,1024]{1,0:T(8,128)(2,1)S(1)}, u32[]{:S(2)}, u32[]{:S(2)}) collective-permute-start(bf16[64,1024]{1,0:T(8,128)(2,1)S(1)} %convert_element_type.39), channel_id=1, source_target_pairs={{0,4},{4,0},{1,5},{5,1},{2,6},{6,2},{3,7},{7,3},{8,12},{12,8},{9,1... | collective-permute-start | bytes 393224 | tf_op jit(solution)/shard_map/ppermute | solution.py:343
  41.4 1.8 %collective-permute-start.5 = (bf16[128,1792]{1,0:T(8,128)(2,1)S(1)}, bf16[128,1792]{1,0:T(8,128)(2,1)S(1)}, u32[]{:S(2)}, u32[]{:S(2)}) collective-permute-start(bf16[128,1792]{1,0:T(8,128)(2,1)S(1)} %get-tuple-element.42), channel_id=1, source_target_pairs={{0,8},{8,0},{16,24},{24,16},{1,9},{9,1},{17,25},{25,17},{2,10},{10... | collective-permute-start | bytes 1376264 | tf_op jit(solution)/shard_map/ppermute | solution.py:342

commit v6 on v5

--- a/solution.py
+++ b/solution.py
@@ -216,8 +216,8 @@
         sigmoid = jax.nn.sigmoid(gate)
         gate_factor_ref[:, columns] = (
             up_rows_ref[:, columns].astype(jnp.float32) * sigmoid * (1.0 + gate * (1.0 - sigmoid))
-        )
-        up_factor_ref[:, columns] = gate * sigmoid
+        ).astype(jnp.bfloat16)
+        up_factor_ref[:, columns] = (gate * sigmoid).astype(jnp.bfloat16)
     for i in range(4):
         weight_copy(i).wait()
         product = jnp.dot(refs[i][...], weight_ref[i], preferred_element_type=jnp.float32)
@@ -238,7 +238,7 @@
     tok_rows = tokens // lax.axis_size("col")
     hidden = jax.ShapeDtypeStruct((tokens, shard), jnp.bfloat16)
     partial = jax.ShapeDtypeStruct((tokens // 2, features), jnp.float32)
-    factor = jax.ShapeDtypeStruct((tok_rows, units), jnp.float32)
+    factor = jax.ShapeDtypeStruct((tok_rows, units), jnp.bfloat16)
     return pl.pallas_call(
         mixed_kernel,
         in_specs=[HBM] * 3 + [VMEM] * 2,
@@ -352,8 +352,8 @@
     )
     so_far = lax.optimization_barrier((so_far, weight_grad))[0]
     hidden_share = so_far + after(from_third, weight_grad, mixed).astype(jnp.float32)
-    gate_grad = (hidden_share * gate_factor).astype(jnp.bfloat16)
-    up_grad = (hidden_share * up_factor).astype(jnp.bfloat16)
+    gate_grad = (hidden_share * gate_factor.astype(jnp.float32)).astype(jnp.bfloat16)
+    up_grad = (hidden_share * up_factor.astype(jnp.float32)).astype(jnp.bfloat16)
     return (mixed, gate_grad, up_grad, weight_grad)
 
 
@@ -380,8 +380,8 @@
         hidden_all, cot_all, (((0,), (0,)), ((), ())), preferred_element_type=jnp.float32
     ) / jnp.float32(lax.axis_size("dp"))
     gate_factor, up_factor = gradient_factors(gate_pre, up_pre)
-    gate_grad = (hidden_share * gate_factor).astype(jnp.bfloat16)
-    up_grad = (hidden_share * up_factor).astype(jnp.bfloat16)
+    gate_grad = (hidden_share * gate_factor.astype(jnp.float32)).astype(jnp.bfloat16)
+    up_grad = (hidden_share * up_factor.astype(jnp.float32)).astype(jnp.bfloat16)
     return (mixed, gate_grad, up_grad, weight_grad)
 
 

time: 49.3 us -> 49.3 us (level)
  no operation moved by 1% of the time
where the time goes in v6:
time: 49.3 us; the launch traced here: 48.9 us
  Pallas kernels  19.6 us (40%)
  starting transfers between devices  15.5 us (31%)
  waiting for transfers between devices  9.81 us (20%)
  other arithmetic  3.29 us (7%)
  between operations  0.76 us (2%)
    pallas_call x1, Pallas kernels, mixed_and_factors(): pl.pallas_call(mixed_kernel, in_specs=[HBM] * 3 + [VMEM] * 2, out_specs=[...  7.74 us
    ppermute x1, waiting for transfers between devices, body_line(): cot_far = lax.ppermute(after(cot_full, mine), 'dp', FAR)  7.22 us
    pallas_call x1, Pallas kernels, hidden_grad_parts(): pl.pallas_call(hidden_grad_kernel, in_specs=[VMEM, VMEM, VMEM, HBM], out_...  4.57 us
    ppermute x1, starting transfers between devices, body_line(): from_end = lax.ppermute(ends, 'col', ENDS)  3.86 us
    pallas_call x1, Pallas kernels, hidden_far_and_weight(): pl.pallas_call(first_kernel, in_specs=[HBM] * 3, out_specs=[VMEM] * 3, ou...  3.74 us
    pallas_call x1, Pallas kernels, weight_grad_shard(): pl.pallas_call(functools.partial(weight_grad_kernel, 0.25), in_specs=[VME...  3.5 us
    ppermute x1, starting transfers between devices, body_line(): from_third = lax.ppermute(forward, 'col', ROUND_THREE)  3.09 us
    ppermute x1, starting transfers between devices, body_line(): cot_other = lax.ppermute(cotangent, 'row', SWAP)  3 us
  transfers between devices with their start and end apart: 11, of which 5 were waited for; matrix products, arithmetic and copies ran while one was open for 4% of the time, Pallas kernels for 31%

profile of v6, /device:TPU:0, one launch (start us, length us, event | category | flops | bytes accessed | tf_op | source)
XLA Modules:
  0.0 48.9 jit_solution(13635861210152737708)
XLA Ops:
  0.6 0.0 copy-start
  0.6 3.0 %collective-permute-start = (bf16[64,1024]{1,0:T(8,128)(2,1)}, bf16[64,1024]{1,0:T(8,128)(2,1)S(1)}, u32[]{:S(2)}, u32[]{:S(2)}) collective-permute-start(bf16[64,1024]{1,0:T(8,128)(2,1)} %own_ref.1), channel_id=1, source_target_pairs={{0,4},{4,0},{1,5},{5,1},{2,6},{6,2},{3,7},{7,3},{8,12},{12,8},{9,1... | collective-permute-start | bytes 393224 | tf_op jit(solution)/shard_map/ppermute | solution.py:318
  3.6 3.7 %hidden_far.1 = (bf16[128,1792]{1,0:T(8,128)(2,1)S(1)}, bf16[128,1792]{1,0:T(8,128)(2,1)S(1)}, bf16[3584,1024]{1,0:T(8,128)(2,1)S(1)}) custom-call(bf16[128,7168]{1,0:T(8,128)(2,1)} %gate_hbm.3, bf16[128,7168]{1,0:T(8,128)(2,1)} %up_hbm.3, bf16[7168,1024]{1,0:T(8,128)(2,1)} %weight_hbm.5), custom_call_target="tpu_custom_call" | custom-call | tf_op jit(solution)/shard_map/hidden_far/pallas_call | solution.py:83
  7.4 0.0 collective-permute-done.other_ref
  7.4 0.0 copy-done
  7.4 4.6 %hidden_grad.1 = (bf16[128,1024]{1,0:T(8,128)(2,1)S(1)}, bf16[32,7168]{1,0:T(8,128)(2,1)S(1)}, bf16[32,7168]{1,0:T(8,128)(2,1)S(1)}, bf16[32,7168]{1,0:T(8,128)(2,1)S(1)}, bf16[32,7168]{1,0:T(8,128)(2,1)S(1)}) custom-call(bf16[64,1024]{1,0:T(8,128)(2,1)S(1)} %copy-done, bf16[64,1024]{1,0:T(8,128)(2,1)S(1)} %collective-permute-done.other_ref, ...), custom_call_target="tpu_custom_call" | custom-call | tf_op jit(solution)/shard_map/hidden_grad/pallas_call | solution.py:150
  12.0 1.4 %collective-permute-start.2 = (bf16[32,7168]{1,0:T(8,128)(2,1)S(1)}, bf16[32,7168]{1,0:T(8,128)(2,1)}, u32[]{:S(2)}, u32[]{:S(2)}) collective-permute-start(bf16[32,7168]{1,0:T(8,128)(2,1)S(1)} %get-tuple-element.34), channel_id=1, source_target_pairs={{1,2},{2,1},{5,6},{6,5},{9,10},{10,9},{13,14},{14,13},{17,18},{18,... | collective-permute-start | bytes 1376264 | tf_op jit(solution)/shard_map/ppermute | solution.py:325
  13.4 3.9 %collective-permute-start.3 = (bf16[32,7168]{1,0:T(8,128)(2,1)S(1)}, bf16[32,7168]{1,0:T(8,128)(2,1)}, u32[]{:S(2)}, u32[]{:S(2)}) collective-permute-start(bf16[32,7168]{1,0:T(8,128)(2,1)S(1)} %get-tuple-element.34), channel_id=1, source_target_pairs={{0,1},{1,0},{2,3},{3,2},{4,5},{5,4},{6,7},{7,6},{8,9},{9,8},{10,11... | collective-permute-start | bytes 1376264 | tf_op jit(solution)/shard_map/ppermute | solution.py:324
  17.3 1.5 %collective-permute-start.1 = (bf16[128,1024]{1,0:T(8,128)(2,1)S(1)}, bf16[128,1024]{1,0:T(8,128)(2,1)S(1)}, u32[]{:S(2)}, u32[]{:S(2)}) collective-permute-start(bf16[128,1024]{1,0:T(8,128)(2,1)S(1)} %get-tuple-element.32.cot_own), channel_id=1, source_target_pairs={{0,16},{8,24},{16,0},{24,8},{1,17},{9,25},{17,1},{25,9},{2,18},{10... | collective-permute-start | bytes 786440 | tf_op jit(solution)/shard_map/ppermute | solution.py:330
  18.8 0.5 %collective-permute-start.4 = (bf16[128,1792]{1,0:T(8,128)(2,1)S(1)}, bf16[128,1792]{1,0:T(8,128)(2,1)S(1)}, u32[]{:S(2)}, u32[]{:S(2)}) collective-permute-start(bf16[128,1792]{1,0:T(8,128)(2,1)S(1)} %get-tuple-element.40.beside_ref), channel_id=1, source_target_pairs={{0,16},{8,24},{16,0},{24,8},{1,17},{9,25},{17,1},{25,9},{2,18},{10... | collective-permute-start | bytes 1376264 | tf_op jit(solution)/shard_map/ppermute | solution.py:328
  19.3 0.0 collective-permute-start.6
  19.3 7.2 %collective-permute-done.1.cot_far = bf16[128,1024]{1,0:T(8,128)(2,1)S(1)} collective-permute-done((bf16[128,1024]{1,0:T(8,128)(2,1)S(1)}, bf16[128,1024]{1,0:T(8,128)(2,1)S(1)}, u32[]{:S(2)}, u32[]{:S(2)}) %collective-permute-start.1) | collective-permute-done | bytes 262176 | tf_op jit(solution)/shard_map/ppermute | solution.py:330
  26.5 0.5 collective-permute-start.9
  27.0 0.0 collective-permute-done.2
  27.0 0.1 collective-permute-start.7
  27.1 1.7 %collective-permute-done.3 = bf16[32,7168]{1,0:T(8,128)(2,1)} collective-permute-done((bf16[32,7168]{1,0:T(8,128)(2,1)S(1)}, bf16[32,7168]{1,0:T(8,128)(2,1)}, u32[]{:S(2)}, u32[]{:S(2)}) %collective-permute-start.3) | collective-permute-done | bytes 458784 | tf_op jit(solution)/shard_map/ppermute | solution.py:324
  28.8 0.1 add_convert_fusion
  29.0 3.1 %collective-permute-start.10 = (bf16[32,7168]{1,0:T(8,128)(2,1)S(1)}, bf16[32,7168]{1,0:T(8,128)(2,1)S(1)}, u32[]{:S(2)}, u32[]{:S(2)}) collective-permute-start(bf16[32,7168]{1,0:T(8,128)(2,1)S(1)} %add_convert_fusion), channel_id=1, source_target_pairs={{0,1},{1,3},{3,2},{2,0},{4,5},{5,7},{7,6},{6,4},{8,9},{9,11},{11,1... | collective-permute-start | bytes 1376264 | tf_op jit(solution)/shard_map/ppermute | solution.py:336
  32.1 7.7 %mixed.1 = (bf16[128,1792]{1,0:T(8,128)(2,1)S(1)}, bf16[128,1792]{1,0:T(8,128)(2,1)S(1)}, f32[64,1024]{1,0:T(8,128)S(1)}, f32[64,1024]{1,0:T(8,128)S(1)}, bf16[3...) custom-call(bf16[128,7168]{1,0:T(8,128)(2,1)} %gate_hbm.3, bf16[128,7168]{1,0:T(8,128)(2,1)} %up_hbm.3, ...), custom_call_target="tpu_custom_call" | custom-call | tf_op jit(solution)/shard_map/mixed/pallas_call | solution.py:242
  39.8 0.0 collective-permute-done.4
  39.8 1.6 %collective-permute-start.8 = (bf16[64,1024]{1,0:T(8,128)(2,1)S(1)}, bf16[64,1024]{1,0:T(8,128)(2,1)S(1)}, u32[]{:S(2)}, u32[]{:S(2)}) collective-permute-start(bf16[64,1024]{1,0:T(8,128)(2,1)S(1)} %convert_element_type.45), channel_id=1, source_target_pairs={{0,4},{4,0},{1,5},{5,1},{2,6},{6,2},{3,7},{7,3},{8,12},{12,8},{9,1... | collective-permute-start | bytes 393224 | tf_op jit(solution)/shard_map/ppermute | solution.py:343
  41.4 0.0 collective-permute-done.9
  41.4 0.0 collective-permute-start.5
  41.4 1.2 %convert_add_fusion.1 = f32[32,7168]{1,0:T(8,128)S(1)} fusion(bf16[32,7168]{1,0:T(8,128)(2,1)S(1)} %collective-permute-done.9, bf16[32,7168]{1,0:T(8,128)(2,1)} %collective-permute-done.2, bf16[32,7168]{1,0:T(8,128)(2,1)S(1)} %get-tuple-element.31), kind=kLoop, calls=%fused_computation.4 | loop fusion | flops 1146880 | bytes 2293760 | tf_op jit(solution)/shard_map/add | solution.py:351
  42.6 0.5 collective-permute-done.6
  43.0 0.2 collective-permute-done.5
  43.2 0.1 pad_maximum_fusion.hidden_ref
  43.3 0.0 collective-permute-done.7.cot_near
  43.4 3.5 %weight_grad.1 = f32[1792,1024]{1,0:T(8,128)} custom-call(bf16[512,1792]{1,0:T(8,128)(2,1)S(1)} %pad_maximum_fusion.hidden_ref, bf16[128,1024]{1,0:T(8,128)(2,1)S(1)} %get-tuple-element.32.cot_own, bf16[128,1024]{1,0:T(8,128)(2,1)S(1)} %collective-permute-done.1.cot_far, bf16[256,1024]{1,0:T(8,128)(2,1)S(1)} %collective-permute-done.7.cot_near), custom_call_target="tpu_custom_call" | custom-call | tf_op jit(solution)/shard_map/weight_grad/pallas_call | solution.py:290
  46.9 0.0 collective-permute-done.8
  46.9 0.7 %add_convert_fusion.1 = bf16[64,1024]{1,0:T(8,128)(2,1)} fusion(f32[64,1024]{1,0:T(8,128)S(1)} %get-tuple-element.44, bf16[64,1024]{1,0:T(8,128)(2,1)S(1)} %collective-permute-done.8), kind=kLoop, calls=%fused_computation.7 | loop fusion | flops 196608 | bytes 524288 | tf_op jit(solution)/shard_map/convert_element_type | solution.py:349
  47.6 0.2 collective-permute-done.10
  47.8 1.1 %multiply_convert_fusion = (bf16[32,7168]{1,0:T(8,128)(2,1)}, bf16[32,7168]{1,0:T(8,128)(2,1)}) fusion(bf16[32,7168]{1,0:T(8,128)(2,1)S(1)} %get-tuple-element.51, f32[32,7168]{1,0:T(8,128)S(1)} %convert_add_fusion.1, bf16[32,7168]{1,0:T(8,128)(2,1)S(1)} %collective-permute-done.10, bf16[32,7168]{1,0:T(8,128)(2,1)S(1)} %get-tuple-element.50), kind=kLoop, calls=%fused_computation.1 | loop fusion | flops 1835008 | bytes 3211264 | tf_op jit(solution)/shard_map/convert_element_type | solution.py:356
  (2 shorter events, 0.1 us)
Async XLA Ops:
  0.6 6.8 %copy-start = (bf16[64,1024]{1,0:T(8,128)(2,1)S(1)}, bf16[64,1024]{1,0:T(8,128)(2,1)}, u32[]{:S(2)}) copy-start(bf16[64,1024]{1,0:T(8,128)(2,1)} %own_ref.1) | copy-start | bytes 393220
  0.6 6.8 %collective-permute-start = (bf16[64,1024]{1,0:T(8,128)(2,1)}, bf16[64,1024]{1,0:T(8,128)(2,1)S(1)}, u32[]{:S(2)}, u32[]{:S(2)}) collective-permute-start(bf16[64,1024]{1,0:T(8,128)(2,1)} %own_ref.1), channel_id=1, source_target_pairs={{0,4},{4,0},{1,5},{5,1},{2,6},{6,2},{3,7},{7,3},{8,12},{12,8},{9,1... | collective-permute-start | bytes 393224 | tf_op jit(solution)/shard_map/ppermute | solution.py:318
  12.0 15.0 %collective-permute-start.2 = (bf16[32,7168]{1,0:T(8,128)(2,1)S(1)}, bf16[32,7168]{1,0:T(8,128)(2,1)}, u32[]{:S(2)}, u32[]{:S(2)}) collective-permute-start(bf16[32,7168]{1,0:T(8,128)(2,1)S(1)} %get-tuple-element.34), channel_id=1, source_target_pairs={{1,2},{2,1},{5,6},{6,5},{9,10},{10,9},{13,14},{14,13},{17,18},{18,... | collective-permute-start | bytes 1376264 | tf_op jit(solution)/shard_map/ppermute | solution.py:325
  13.4 15.4 %collective-permute-start.3 = (bf16[32,7168]{1,0:T(8,128)(2,1)S(1)}, bf16[32,7168]{1,0:T(8,128)(2,1)}, u32[]{:S(2)}, u32[]{:S(2)}) collective-permute-start(bf16[32,7168]{1,0:T(8,128)(2,1)S(1)} %get-tuple-element.34), channel_id=1, source_target_pairs={{0,1},{1,0},{2,3},{3,2},{4,5},{5,4},{6,7},{7,6},{8,9},{9,8},{10,11... | collective-permute-start | bytes 1376264 | tf_op jit(solution)/shard_map/ppermute | solution.py:324
  17.3 9.2 %collective-permute-start.1 = (bf16[128,1024]{1,0:T(8,128)(2,1)S(1)}, bf16[128,1024]{1,0:T(8,128)(2,1)S(1)}, u32[]{:S(2)}, u32[]{:S(2)}) collective-permute-start(bf16[128,1024]{1,0:T(8,128)(2,1)S(1)} %get-tuple-element.32.cot_own), channel_id=1, source_target_pairs={{0,16},{8,24},{16,0},{24,8},{1,17},{9,25},{17,1},{25,9},{2,18},{10... | collective-permute-start | bytes 786440 | tf_op jit(solution)/shard_map/ppermute | solution.py:330
  18.8 21.0 %collective-permute-start.4 = (bf16[128,1792]{1,0:T(8,128)(2,1)S(1)}, bf16[128,1792]{1,0:T(8,128)(2,1)S(1)}, u32[]{:S(2)}, u32[]{:S(2)}) collective-permute-start(bf16[128,1792]{1,0:T(8,128)(2,1)S(1)} %get-tuple-element.40.beside_ref), channel_id=1, source_target_pairs={{0,16},{8,24},{16,0},{24,8},{1,17},{9,25},{17,1},{25,9},{2,18},{10... | collective-permute-start | bytes 1376264 | tf_op jit(solution)/shard_map/ppermute | solution.py:328
  19.3 23.7 %collective-permute-start.6 = (bf16[128,1792]{1,0:T(8,128)(2,1)S(1)}, bf16[128,1792]{1,0:T(8,128)(2,1)S(1)}, u32[]{:S(2)}, u32[]{:S(2)}) collective-permute-start(bf16[128,1792]{1,0:T(8,128)(2,1)S(1)} %get-tuple-element.43.across_ref), channel_id=1, source_target_pairs={{0,24},{8,16},{16,8},{24,0},{1,25},{9,17},{17,9},{25,1},{2,26},{10... | collective-permute-start | bytes 1376264 | tf_op jit(solution)/shard_map/ppermute | solution.py:327
  26.5 14.9 %collective-permute-start.9 = (bf16[32,7168]{1,0:T(8,128)(2,1)S(1)}, bf16[32,7168]{1,0:T(8,128)(2,1)S(1)}, u32[]{:S(2)}, u32[]{:S(2)}) collective-permute-start(bf16[32,7168]{1,0:T(8,128)(2,1)S(1)} %get-tuple-element.47), channel_id=1, source_target_pairs={{0,2},{2,3},{3,1},{1,0},{4,6},{6,7},{7,5},{5,4},{8,10},{10,11},{11... | collective-permute-start | bytes 1376264 | tf_op jit(solution)/shard_map/ppermute | solution.py:326
  27.0 16.3 %collective-permute-start.7 = (bf16[256,1024]{1,0:T(8,128)(2,1)S(1)}, bf16[256,1024]{1,0:T(8,128)(2,1)S(1)}, u32[]{:S(2)}, u32[]{:S(2)}) collective-permute-start(bf16[256,1024]{1,0:T(8,128)(2,1)S(1)} %pad_maximum_fusion.1), channel_id=1, source_target_pairs={{0,8},{8,0},{16,24},{24,16},{1,9},{9,1},{17,25},{25,17},{2,10},{10... | collective-permute-start | bytes 1572872 | tf_op jit(solution)/shard_map/ppermute | solution.py:341
  29.0 18.8 %collective-permute-start.10 = (bf16[32,7168]{1,0:T(8,128)(2,1)S(1)}, bf16[32,7168]{1,0:T(8,128)(2,1)S(1)}, u32[]{:S(2)}, u32[]{:S(2)}) collective-permute-start(bf16[32,7168]{1,0:T(8,128)(2,1)S(1)} %add_convert_fusion), channel_id=1, source_target_pairs={{0,1},{1,3},{3,2},{2,0},{4,5},{5,7},{7,6},{6,4},{8,9},{9,11},{11,1... | collective-permute-start | bytes 1376264 | tf_op jit(solution)/shard_map/ppermute | solution.py:336
  39.8 7.0 %collective-permute-start.8 = (bf16[64,1024]{1,0:T(8,128)(2,1)S(1)}, bf16[64,1024]{1,0:T(8,128)(2,1)S(1)}, u32[]{:S(2)}, u32[]{:S(2)}) collective-permute-start(bf16[64,1024]{1,0:T(8,128)(2,1)S(1)} %convert_element_type.45), channel_id=1, source_target_pairs={{0,4},{4,0},{1,5},{5,1},{2,6},{6,2},{3,7},{7,3},{8,12},{12,8},{9,1... | collective-permute-start | bytes 393224 | tf_op jit(solution)/shard_map/ppermute | solution.py:343
  41.4 1.8 %collective-permute-start.5 = (bf16[128,1792]{1,0:T(8,128)(2,1)S(1)}, bf16[128,1792]{1,0:T(8,128)(2,1)S(1)}, u32[]{:S(2)}, u32[]{:S(2)}) collective-permute-start(bf16[128,1792]{1,0:T(8,128)(2,1)S(1)} %get-tuple-element.42), channel_id=1, source_target_pairs={{0,8},{8,0},{16,24},{24,16},{1,9},{9,1},{17,25},{25,17},{2,10},{10... | collective-permute-start | bytes 1376264 | tf_op jit(solution)/shard_map/ppermute | solution.py:342
